TPU v7x, 512 devices: a whole 4x4x16 slice. The times are simulated.
512 devices in a mesh: gx: 64 (over x, z_lo, core), gy: 8 (over y, z_hi).
Axes of the slice: x: 4, y: 4, z: 16 (z_hi: 2, z_lo: 8; z = z_hi * 8 + z_lo), core: 2. Of those that a mesh axis runs over, the one named last changes fastest.
Arguments:
- directions: float32 [16, 4096, 1024], P(None, 'gx', 'gy'), may hold values from -6 to 6
- east_speed: float32 [4096, 1024], P('gx', 'gy'), may hold values from -0.25 to 0.25
- north_speed: float32 [4096, 1024], P('gx', 'gy'), may hold values from -0.25 to 0.25
- diffusion: float32 [4096, 1024], P('gx', 'gy'), may hold values from 0.01 to 0.08
- precision: float32 [4096, 1024], P('gx', 'gy'), may hold values from 6 to 162, as said below
Outputs:
- basis: float32 [16, 4096, 1024], P(None, 'gx', 'gy')
- factor: float32 [16, 16], replicated
Inputs may be any that keep to these rules, and one draw needn't show every extreme that they name: `precision`: positive.
All inputs are finite; a program needn't handle non-finite values.
Results may differ from a plain program's by a relative error of at most 0.0003.
Values sent between devices are 32-bit elements; how exact they have to be, the bound alone decides.
A program may use at most 64 MiB of HBM per device.

v0:
```python
import math

import jax
import jax.numpy as jnp
from jax import lax
from jax.sharding import PartitionSpec as P

STEPS = 4


def extended(value, sides, width, wrap):
    for axis, dim in sides:
        size, length = (lax.axis_size(axis), value.shape[dim])
        up = [(i, (i + 1) % size) for i in range(size if wrap else size - 1)]
        down = [(j, i) for i, j in up]
        last = lax.slice_in_dim(value, length - width, length, axis=dim)
        leading = lax.slice_in_dim(value, 0, width, axis=dim)
        before = lax.ppermute(last, axis, up)
        after = lax.ppermute(leading, axis, down)
        value = jnp.concatenate([before, value, after], axis=dim)
    return value


def extend_field(field, depth):
    wider = extended(field, (("gx", 1),), depth, True)
    return extended(wider, (("gy", 2),), depth, False)


def extend_coefs(stacked, depth):
    wider = extended(stacked, (("gx", 1),), depth, True)
    return extended(wider, (("gy", 2),), depth, False)


def trim_rim(array, margin):
    return array[:, margin : array.shape[1] - margin, margin : array.shape[2] - margin]


def forward_step(padded, coefs):
    return (
        coefs[0] * padded[:, 1:-1, 1:-1]
        + coefs[1] * padded[:, 2:, 1:-1]
        + coefs[2] * padded[:, :-2, 1:-1]
        + coefs[3] * padded[:, 1:-1, 2:]
        + coefs[4] * padded[:, 1:-1, :-2]
    )


def adjoint_step(padded, coefs):
    inner = (
        coefs[0, 1:-1, 1:-1] * padded[:, 1:-1, 1:-1]
        + coefs[1, :-2, 1:-1] * padded[:, :-2, 1:-1]
        + coefs[2, 2:, 1:-1] * padded[:, 2:, 1:-1]
        + coefs[3, 1:-1, :-2] * padded[:, 1:-1, :-2]
        + coefs[4, 1:-1, 2:] * padded[:, 1:-1, 2:]
    )
    return inner * coefs[5, 1:-1, 1:-1]


def per_device(directions, east_speed, north_speed, diffusion, precision):
    east = diffusion + jnp.maximum(-east_speed, 0.0)
    west = diffusion + jnp.maximum(east_speed, 0.0)
    north = diffusion + jnp.maximum(-north_speed, 0.0)
    south = diffusion + jnp.maximum(north_speed, 0.0)
    centre = 1.0 - east - west - north - south
    stacked = jnp.stack([centre, east, west, north, south, jnp.ones_like(centre)])
    depth = 1
    coef_pad = extend_coefs(stacked, depth)
    field = directions
    for block in range(STEPS // depth):
        padded = extend_field(field, depth)
        inner = 0
        padded = forward_step(padded, trim_rim(coef_pad, inner + 1))
        field = padded
    field = precision * field
    for block in range(STEPS // depth):
        padded = extend_field(field, depth)
        inner = 0
        padded = adjoint_step(padded, trim_rim(coef_pad, inner))
        field = padded
    rows_x = field.shape[1]
    rows_y = field.shape[2]
    flat = field.reshape(field.shape[0], rows_x * rows_y)
    local_gram = jnp.dot(flat, flat.T, precision=lax.Precision.HIGHEST)
    gram = lax.psum(local_gram, ("gx", "gy"))
    lower = jnp.linalg.cholesky(gram)
    solved = lax.linalg.triangular_solve(lower, flat, left_side=True, lower=True)
    scale = math.sqrt(float(rows_x * rows_y * lax.axis_size("gx") * lax.axis_size("gy")))
    basis = (solved * scale).reshape(field.shape)
    factor = lower.T / scale
    return (basis, factor)


def solution(mesh):
    return jax.shard_map(
        per_device,
        mesh=mesh,
        in_specs=(P(None, "gx", "gy"), P("gx", "gy"), P("gx", "gy"), P("gx", "gy"), P("gx", "gy")),
        out_specs=(P(None, "gx", "gy"), P()),
        check_vma=False,
    )
```

profile of v0, /device:TPU:1, one launch (start us, length us, event | category | flops | bytes accessed | tf_op | source)
XLA Modules:
  0.0 497.8 jit_solution(8323854215730433228)
XLA Ops:
  1.5 8.8 %collective-permute-start = (f32[16,1,128]{2,0,1:T(8,128)S(1)}, f32[16,1,128]{2,0,1:T(8,128)S(1)}, u32[]{:S(2)}, u32[]{:S(2)}) collective-permute-start(f32[16,1,128]{2,0,1:T(8,128)S(1)} %bitcast.44), channel_id=1, source_target_pairs={{8,0},{16,8},{24,16},{32,24},{40,32},{48,40},{56,48},{64,56},{72,6... | collective-permute-start | bytes 24584 | tf_op jit(solution)/shard_map/ppermute | solution.py:19
  10.3 1.9 collective-permute-start.1
  12.3 1.4 bitcast_dynamic-update-slice_fusion.4
  13.7 1.5 copy.55
  15.2 5.2 %collective-permute-done.1 = f32[16,1,128]{2,0,1:T(8,128)S(1)} collective-permute-done((f32[16,1,128]{2,0,1:T(8,128)S(1)}, f32[16,1,128]{2,0,1:T(8,128)S(1)}, u32[]{:S(2)}, u32[]{:S(2)}) %collective-permute-start.1) | collective-permute-done | bytes 8224 | tf_op jit(solution)/shard_map/ppermute | solution.py:18
  23.7 12.7 %collective-permute-start.3 = (f32[16,66,1]{1,0,2:T(8,128)S(1)}, f32[16,66,1]{1,0,2:T(8,128)S(1)}, u32[]{:S(2)}, u32[]{:S(2)}) collective-permute-start(f32[16,66,1]{1,0,2:T(8,128)S(1)} %get-tuple-element.31), channel_id=1, source_target_pairs={{0,1},{1,2},{2,3},{3,4},{4,5},{5,6},{6,7},{8,9},{9,10},{10,11},{11... | collective-permute-start | bytes 12680 | tf_op jit(solution)/shard_map/ppermute | solution.py:18
  38.9 3.9 fusion.59
  44.0 13.6 %collective-permute-start.4 = (f32[16,1,128]{2,0,1:T(8,128)S(1)}, f32[16,1,128]{2,0,1:T(8,128)S(1)}, u32[]{:S(2)}, u32[]{:S(2)}) collective-permute-start(f32[16,1,128]{2,0,1:T(8,128)S(1)} %copy.69), channel_id=1, source_target_pairs={{8,0},{16,8},{24,16},{32,24},{40,32},{48,40},{56,48},{64,56},{72,6... | collective-permute-start | bytes 24584 | tf_op jit(solution)/shard_map/ppermute | solution.py:19
  57.6 1.9 collective-permute-start.5
  64.6 12.7 %collective-permute-start.7 = (f32[16,66,1]{1,0,2:T(8,128)S(1)}, f32[16,66,1]{1,0,2:T(8,128)S(1)}, u32[]{:S(2)}, u32[]{:S(2)}) collective-permute-start(f32[16,66,1]{1,0,2:T(8,128)S(1)} %get-tuple-element.29), channel_id=1, source_target_pairs={{0,1},{1,2},{2,3},{3,4},{4,5},{5,6},{6,7},{8,9},{9,10},{10,11},{11... | collective-permute-start | bytes 12680 | tf_op jit(solution)/shard_map/ppermute | solution.py:18
  78.1 3.9 fusion.51
  83.3 14.2 %collective-permute-start.8 = (f32[16,1,128]{2,0,1:T(8,128)S(1)}, f32[16,1,128]{2,0,1:T(8,128)S(1)}, u32[]{:S(2)}, u32[]{:S(2)}) collective-permute-start(f32[16,1,128]{2,0,1:T(8,128)S(1)} %copy.75), channel_id=1, source_target_pairs={{8,0},{16,8},{24,16},{32,24},{40,32},{48,40},{56,48},{64,56},{72,6... | collective-permute-start | bytes 24584 | tf_op jit(solution)/shard_map/ppermute | solution.py:19
  97.5 1.9 collective-permute-start.9
  103.8 13.7 %collective-permute-start.11 = (f32[16,66,1]{1,0,2:T(8,128)S(1)}, f32[16,66,1]{1,0,2:T(8,128)S(1)}, u32[]{:S(2)}, u32[]{:S(2)}) collective-permute-start(f32[16,66,1]{1,0,2:T(8,128)S(1)} %get-tuple-element.27), channel_id=1, source_target_pairs={{0,1},{1,2},{2,3},{3,4},{4,5},{5,6},{6,7},{8,9},{9,10},{10,11},{11... | collective-permute-start | bytes 12680 | tf_op jit(solution)/shard_map/ppermute | solution.py:18
  118.2 3.9 fusion.43
  123.4 13.1 %collective-permute-start.12 = (f32[16,1,128]{2,0,1:T(8,128)S(1)}, f32[16,1,128]{2,0,1:T(8,128)S(1)}, u32[]{:S(2)}, u32[]{:S(2)}) collective-permute-start(f32[16,1,128]{2,0,1:T(8,128)S(1)} %copy.81), channel_id=1, source_target_pairs={{8,0},{16,8},{24,16},{32,24},{40,32},{48,40},{56,48},{64,56},{72,6... | collective-permute-start | bytes 24584 | tf_op jit(solution)/shard_map/ppermute | solution.py:19
  136.4 1.9 collective-permute-start.13
  139.1 1.9 collective-permute-start.16
  141.1 2.4 collective-permute-start.18
  147.6 14.0 %collective-permute-start.15 = (f32[16,66,1]{1,0,2:T(8,128)S(1)}, f32[16,66,1]{1,0,2:T(8,128)S(1)}, u32[]{:S(2)}, u32[]{:S(2)}) collective-permute-start(f32[16,66,1]{1,0,2:T(8,128)S(1)} %get-tuple-element.25), channel_id=1, source_target_pairs={{0,1},{1,2},{2,3},{3,4},{4,5},{5,6},{6,7},{8,9},{9,10},{10,11},{11... | collective-permute-start | bytes 12680 | tf_op jit(solution)/shard_map/ppermute | solution.py:18
  162.4 3.9 fusion.35
  167.5 13.2 %collective-permute-start.19 = (f32[16,1,128]{2,0,1:T(8,128)S(1)}, f32[16,1,128]{2,0,1:T(8,128)S(1)}, u32[]{:S(2)}, u32[]{:S(2)}) collective-permute-start(f32[16,1,128]{2,0,1:T(8,128)S(1)} %copy.91), channel_id=1, source_target_pairs={{8,0},{16,8},{24,16},{32,24},{40,32},{48,40},{56,48},{64,56},{72,6... | collective-permute-start | bytes 24584 | tf_op jit(solution)/shard_map/ppermute | solution.py:19
  180.7 1.9 collective-permute-start.17
  183.5 13.5 %collective-permute-start.20 = (f32[6,66,1]{2,1,0:T(8,128)}, f32[6,66,1]{2,1,0:T(8,128)S(1)}, u32[]{:S(2)}, u32[]{:S(2)}) collective-permute-start(f32[6,66,1]{2,1,0:T(8,128)} %get-tuple-element.48), channel_id=1, source_target_pairs={{0,1},{1,2},{2,3},{3,4},{4,5},{5,6},{6,7},{8,9},{9,10},{10,11},{11... | collective-permute-start | bytes 4760 | tf_op jit(solution)/shard_map/ppermute | solution.py:18
  197.0 1.3 collective-permute-start.22
  200.4 14.6 %collective-permute-start.21 = (f32[16,66,1]{1,0,2:T(8,128)S(1)}, f32[16,66,1]{1,0,2:T(8,128)S(1)}, u32[]{:S(2)}, u32[]{:S(2)}) collective-permute-start(f32[16,66,1]{1,0,2:T(8,128)S(1)} %get-tuple-element.22), channel_id=1, source_target_pairs={{0,1},{1,2},{2,3},{3,4},{4,5},{5,6},{6,7},{8,9},{9,10},{10,11},{11... | collective-permute-start | bytes 12680 | tf_op jit(solution)/shard_map/ppermute | solution.py:18
  216.3 2.9 collective-permute-done.22
  220.5 8.5 %collective-permute-done.23 = f32[16,66,1]{1,0,2:T(8,128)S(1)} collective-permute-done((f32[16,66,1]{1,0,2:T(8,128)S(1)}, f32[16,66,1]{1,0,2:T(8,128)S(1)}, u32[]{:S(2)}, u32[]{:S(2)}) %collective-permute-start.23) | collective-permute-done | bytes 4256 | tf_op jit(solution)/shard_map/ppermute | solution.py:19
  229.0 4.0 fusion.26
  233.8 2.1 collective-permute-start.24
  236.4 4.1 collective-permute-start.25
  242.9 13.2 %collective-permute-start.26 = (f32[16,66,1]{1,0,2:T(8,128)S(1)}, f32[16,66,1]{1,0,2:T(8,128)S(1)}, u32[]{:S(2)}, u32[]{:S(2)}) collective-permute-start(f32[16,66,1]{1,0,2:T(8,128)S(1)} %get-tuple-element.20), channel_id=1, source_target_pairs={{0,1},{1,2},{2,3},{3,4},{4,5},{5,6},{6,7},{8,9},{9,10},{10,11},{11... | collective-permute-start | bytes 12680 | tf_op jit(solution)/shard_map/ppermute | solution.py:18
  257.4 11.8 %collective-permute-done.27 = f32[16,66,1]{1,0,2:T(8,128)S(1)} collective-permute-done((f32[16,66,1]{1,0,2:T(8,128)S(1)}, f32[16,66,1]{1,0,2:T(8,128)S(1)}, u32[]{:S(2)}, u32[]{:S(2)}) %collective-permute-start.27) | collective-permute-done | bytes 4256 | tf_op jit(solution)/shard_map/ppermute | solution.py:19
  269.2 4.1 fusion.18
  274.1 3.1 collective-permute-start.28
  277.6 13.1 %collective-permute-start.29 = (f32[16,1,128]{2,0,1:T(8,128)S(1)}, f32[16,1,128]{2,0,1:T(8,128)S(1)}, u32[]{:S(2)}, u32[]{:S(2)}) collective-permute-start(f32[16,1,128]{2,0,1:T(8,128)S(1)} %copy.105), channel_id=1, source_target_pairs={{8,0},{16,8},{24,16},{32,24},{40,32},{48,40},{56,48},{64,56},{72,6... | collective-permute-start | bytes 24584 | tf_op jit(solution)/shard_map/ppermute | solution.py:19
  293.1 11.9 %collective-permute-start.30 = (f32[16,66,1]{1,0,2:T(8,128)S(1)}, f32[16,66,1]{1,0,2:T(8,128)S(1)}, u32[]{:S(2)}, u32[]{:S(2)}) collective-permute-start(f32[16,66,1]{1,0,2:T(8,128)S(1)} %get-tuple-element.18), channel_id=1, source_target_pairs={{0,1},{1,2},{2,3},{3,4},{4,5},{5,6},{6,7},{8,9},{9,10},{10,11},{11... | collective-permute-start | bytes 12680 | tf_op jit(solution)/shard_map/ppermute | solution.py:18
  306.3 12.1 %collective-permute-done.31 = f32[16,66,1]{1,0,2:T(8,128)S(1)} collective-permute-done((f32[16,66,1]{1,0,2:T(8,128)S(1)}, f32[16,66,1]{1,0,2:T(8,128)S(1)}, u32[]{:S(2)}, u32[]{:S(2)}) %collective-permute-start.31) | collective-permute-done | bytes 4256 | tf_op jit(solution)/shard_map/ppermute | solution.py:19
  318.4 4.1 fusion.10
  323.2 1.9 collective-permute-start.32
  325.6 14.0 %collective-permute-start.33 = (f32[16,1,128]{2,0,1:T(8,128)S(1)}, f32[16,1,128]{2,0,1:T(8,128)S(1)}, u32[]{:S(2)}, u32[]{:S(2)}) collective-permute-start(f32[16,1,128]{2,0,1:T(8,128)S(1)} %copy.111), channel_id=1, source_target_pairs={{8,0},{16,8},{24,16},{32,24},{40,32},{48,40},{56,48},{64,56},{72,6... | collective-permute-start | bytes 24584 | tf_op jit(solution)/shard_map/ppermute | solution.py:19
  342.0 13.2 %collective-permute-start.34 = (f32[16,66,1]{1,0,2:T(8,128)S(1)}, f32[16,66,1]{1,0,2:T(8,128)S(1)}, u32[]{:S(2)}, u32[]{:S(2)}) collective-permute-start(f32[16,66,1]{1,0,2:T(8,128)S(1)} %get-tuple-element.16), channel_id=1, source_target_pairs={{0,1},{1,2},{2,3},{3,4},{4,5},{5,6},{6,7},{8,9},{9,10},{10,11},{11... | collective-permute-start | bytes 12680 | tf_op jit(solution)/shard_map/ppermute | solution.py:18
  355.2 1.5 collective-permute-start.35
  356.8 11.6 %collective-permute-done.35 = f32[16,66,1]{1,0,2:T(8,128)S(1)} collective-permute-done((f32[16,66,1]{1,0,2:T(8,128)S(1)}, f32[16,66,1]{1,0,2:T(8,128)S(1)}, u32[]{:S(2)}, u32[]{:S(2)}) %collective-permute-start.35) | collective-permute-done | bytes 4256 | tf_op jit(solution)/shard_map/ppermute | solution.py:19
  368.3 4.1 fusion.2
  372.4 1.5 convolution_bitcast_fusion
  374.4 116.7 %psum.7 = f32[16,16]{0,1:T(8,128)S(1)} all-reduce(f32[16,16]{0,1:T(8,128)S(1)} %convolution_bitcast_fusion), channel_id=1, replica_groups=mesh['gx'=64,'gy'=8] {'gx','gy'}, use_global_device_ids=true, to_apply=%region_0.0 | all-reduce | flops 256 | bytes 2048 | tf_op jit(solution)/shard_map/psum | solution.py:84
  491.1 1.5 cholesky.16
  (162 shorter events, 52.0 us)
Async XLA Ops:
  1.5 19.4 %collective-permute-start = (f32[16,1,128]{2,0,1:T(8,128)S(1)}, f32[16,1,128]{2,0,1:T(8,128)S(1)}, u32[]{:S(2)}, u32[]{:S(2)}) collective-permute-start(f32[16,1,128]{2,0,1:T(8,128)S(1)} %bitcast.44), channel_id=1, source_target_pairs={{8,0},{16,8},{24,16},{32,24},{40,32},{48,40},{56,48},{64,56},{72,6... | collective-permute-start | bytes 24584 | tf_op jit(solution)/shard_map/ppermute | solution.py:19
  10.3 10.1 %collective-permute-start.1 = (f32[16,1,128]{2,0,1:T(8,128)S(1)}, f32[16,1,128]{2,0,1:T(8,128)S(1)}, u32[]{:S(2)}, u32[]{:S(2)}) collective-permute-start(f32[16,1,128]{2,0,1:T(8,128)S(1)} %bitcast.45), channel_id=1, source_target_pairs={{0,8},{8,16},{16,24},{24,32},{32,40},{40,48},{48,56},{56,64},{64,7... | collective-permute-start | bytes 24584 | tf_op jit(solution)/shard_map/ppermute | solution.py:18
  13.7 23.6 %copy-start.17 = (f32[64,128]{1,0:T(8,128)}, f32[64,128]{1,0:T(8,128)S(1)}, u32[]{:S(2)}) copy-start(f32[64,128]{1,0:T(8,128)S(1)} %get-tuple-element.14) | copy-start | bytes 98308
  22.4 16.4 %collective-permute-start.2 = (f32[16,66,1]{1,0,2:T(8,128)S(1)}, f32[16,66,1]{1,0,2:T(8,128)S(1)}, u32[]{:S(2)}, u32[]{:S(2)}) collective-permute-start(f32[16,66,1]{1,0,2:T(8,128)S(1)} %get-tuple-element.30), channel_id=1, source_target_pairs={{1,0},{2,1},{3,2},{4,3},{5,4},{6,5},{7,6},{9,8},{10,9},{11,10},{12... | collective-permute-start | bytes 12680 | tf_op jit(solution)/shard_map/ppermute | solution.py:19
  23.7 15.2 %collective-permute-start.3 = (f32[16,66,1]{1,0,2:T(8,128)S(1)}, f32[16,66,1]{1,0,2:T(8,128)S(1)}, u32[]{:S(2)}, u32[]{:S(2)}) collective-permute-start(f32[16,66,1]{1,0,2:T(8,128)S(1)} %get-tuple-element.31), channel_id=1, source_target_pairs={{0,1},{1,2},{2,3},{3,4},{4,5},{5,6},{6,7},{8,9},{9,10},{10,11},{11... | collective-permute-start | bytes 12680 | tf_op jit(solution)/shard_map/ppermute | solution.py:18
  37.2 81.0 %copy-start.8 = (f32[64,128]{0,1:T(8,128)}, f32[64,128]{0,1:T(8,128)S(1)}, u32[]{:S(2)}) copy-start(f32[64,128]{0,1:T(8,128)S(1)} %copy.68) | copy-start | bytes 98308
  37.4 80.8 %copy-start.10 = (f32[64,128]{0,1:T(8,128)}, f32[64,128]{0,1:T(8,128)S(1)}, u32[]{:S(2)}) copy-start(f32[64,128]{0,1:T(8,128)S(1)} %copy.64) | copy-start | bytes 98308
  38.1 80.1 %copy-start.12 = (f32[64,128]{0,1:T(8,128)}, f32[64,128]{0,1:T(8,128)S(1)}, u32[]{:S(2)}) copy-start(f32[64,128]{0,1:T(8,128)S(1)} %copy.60) | copy-start | bytes 98308
  43.6 16.0 %copy-start.20 = (f32[64,128]{1,0:T(8,128)S(1)}, f32[64,128]{1,0:T(8,128)}, u32[]{:S(2)}) copy-start(f32[64,128]{1,0:T(8,128)} %get-tuple-element.13) | copy-start | bytes 98308
  44.0 17.8 %collective-permute-start.4 = (f32[16,1,128]{2,0,1:T(8,128)S(1)}, f32[16,1,128]{2,0,1:T(8,128)S(1)}, u32[]{:S(2)}, u32[]{:S(2)}) collective-permute-start(f32[16,1,128]{2,0,1:T(8,128)S(1)} %copy.69), channel_id=1, source_target_pairs={{8,0},{16,8},{24,16},{32,24},{40,32},{48,40},{56,48},{64,56},{72,6... | collective-permute-start | bytes 24584 | tf_op jit(solution)/shard_map/ppermute | solution.py:19
  57.6 3.7 collective-permute-start.5
  62.4 15.0 %copy-start.18 = (f32[64,128]{1,0:T(8,128)S(1)}, f32[64,128]{1,0:T(8,128)}, u32[]{:S(2)}) copy-start(f32[64,128]{1,0:T(8,128)} %copy-done.17) | copy-start | bytes 98308
  63.4 14.6 %collective-permute-start.6 = (f32[16,66,1]{1,0,2:T(8,128)S(1)}, f32[16,66,1]{1,0,2:T(8,128)S(1)}, u32[]{:S(2)}, u32[]{:S(2)}) collective-permute-start(f32[16,66,1]{1,0,2:T(8,128)S(1)} %get-tuple-element.28), channel_id=1, source_target_pairs={{1,0},{2,1},{3,2},{4,3},{5,4},{6,5},{7,6},{9,8},{10,9},{11,10},{12... | collective-permute-start | bytes 12680 | tf_op jit(solution)/shard_map/ppermute | solution.py:19
  64.6 13.5 %collective-permute-start.7 = (f32[16,66,1]{1,0,2:T(8,128)S(1)}, f32[16,66,1]{1,0,2:T(8,128)S(1)}, u32[]{:S(2)}, u32[]{:S(2)}) collective-permute-start(f32[16,66,1]{1,0,2:T(8,128)S(1)} %get-tuple-element.29), channel_id=1, source_target_pairs={{0,1},{1,2},{2,3},{3,4},{4,5},{5,6},{6,7},{8,9},{9,10},{10,11},{11... | collective-permute-start | bytes 12680 | tf_op jit(solution)/shard_map/ppermute | solution.py:18
  83.3 17.8 %collective-permute-start.8 = (f32[16,1,128]{2,0,1:T(8,128)S(1)}, f32[16,1,128]{2,0,1:T(8,128)S(1)}, u32[]{:S(2)}, u32[]{:S(2)}) collective-permute-start(f32[16,1,128]{2,0,1:T(8,128)S(1)} %copy.75), channel_id=1, source_target_pairs={{8,0},{16,8},{24,16},{32,24},{40,32},{48,40},{56,48},{64,56},{72,6... | collective-permute-start | bytes 24584 | tf_op jit(solution)/shard_map/ppermute | solution.py:19
  97.5 3.1 collective-permute-start.9
  102.6 15.6 %collective-permute-start.10 = (f32[16,66,1]{1,0,2:T(8,128)S(1)}, f32[16,66,1]{1,0,2:T(8,128)S(1)}, u32[]{:S(2)}, u32[]{:S(2)}) collective-permute-start(f32[16,66,1]{1,0,2:T(8,128)S(1)} %get-tuple-element.26), channel_id=1, source_target_pairs={{1,0},{2,1},{3,2},{4,3},{5,4},{6,5},{7,6},{9,8},{10,9},{11,10},{12... | collective-permute-start | bytes 12680 | tf_op jit(solution)/shard_map/ppermute | solution.py:19
  103.8 14.3 %collective-permute-start.11 = (f32[16,66,1]{1,0,2:T(8,128)S(1)}, f32[16,66,1]{1,0,2:T(8,128)S(1)}, u32[]{:S(2)}, u32[]{:S(2)}) collective-permute-start(f32[16,66,1]{1,0,2:T(8,128)S(1)} %get-tuple-element.27), channel_id=1, source_target_pairs={{0,1},{1,2},{2,3},{3,4},{4,5},{5,6},{6,7},{8,9},{9,10},{10,11},{11... | collective-permute-start | bytes 12680 | tf_op jit(solution)/shard_map/ppermute | solution.py:18
  122.9 20.5 %copy-start.24 = (f32[64,128]{1,0:T(8,128)S(1)}, f32[64,128]{1,0:T(8,128)}, u32[]{:S(2)}) copy-start(f32[64,128]{1,0:T(8,128)} %param.9) | copy-start | bytes 98308
  123.4 21.4 %collective-permute-start.12 = (f32[16,1,128]{2,0,1:T(8,128)S(1)}, f32[16,1,128]{2,0,1:T(8,128)S(1)}, u32[]{:S(2)}, u32[]{:S(2)}) collective-permute-start(f32[16,1,128]{2,0,1:T(8,128)S(1)} %copy.81), channel_id=1, source_target_pairs={{8,0},{16,8},{24,16},{32,24},{40,32},{48,40},{56,48},{64,56},{72,6... | collective-permute-start | bytes 24584 | tf_op jit(solution)/shard_map/ppermute | solution.py:19
  136.4 7.8 %collective-permute-start.13 = (f32[16,1,128]{2,0,1:T(8,128)S(1)}, f32[16,1,128]{2,0,1:T(8,128)S(1)}, u32[]{:S(2)}, u32[]{:S(2)}) collective-permute-start(f32[16,1,128]{2,0,1:T(8,128)S(1)} %copy.83), channel_id=1, source_target_pairs={{0,8},{8,16},{16,24},{24,32},{32,40},{40,48},{48,56},{56,64},{64,7... | collective-permute-start | bytes 24584 | tf_op jit(solution)/shard_map/ppermute | solution.py:18
  139.1 22.5 %collective-permute-start.16 = (f32[6,1,128]{2,1,0:T(1,128)S(1)}, f32[6,1,128]{2,1,0:T(1,128)S(1)}, u32[]{:S(2)}, u32[]{:S(2)}) collective-permute-start(f32[6,1,128]{2,1,0:T(1,128)S(1)} %get-tuple-element.54), channel_id=1, source_target_pairs={{0,8},{8,16},{16,24},{24,32},{32,40},{40,48},{48,56},{56,64},{64,7... | collective-permute-start | bytes 9224 | tf_op jit(solution)/shard_map/ppermute | solution.py:18
  141.1 20.5 %collective-permute-start.18 = (f32[6,1,128]{2,1,0:T(1,128)S(1)}, f32[6,1,128]{2,1,0:T(1,128)S(1)}, u32[]{:S(2)}, u32[]{:S(2)}) collective-permute-start(f32[6,1,128]{2,1,0:T(1,128)S(1)} %get-tuple-element.55), channel_id=1, source_target_pairs={{8,0},{16,8},{24,16},{32,24},{40,32},{48,40},{56,48},{64,56},{72,6... | collective-permute-start | bytes 9224 | tf_op jit(solution)/shard_map/ppermute | solution.py:19
  145.3 16.3 %copy-start.15 = (f32[6,64,128]{2,1,0:T(8,128)S(1)}, f32[6,64,128]{2,1,0:T(8,128)}, u32[]{:S(2)}) copy-start(f32[6,64,128]{2,1,0:T(8,128)} %broadcast_dynamic-update-slice_fusion) | copy-start | bytes 589828
  146.2 15.4 %collective-permute-start.14 = (f32[16,66,1]{1,0,2:T(8,128)S(1)}, f32[16,66,1]{1,0,2:T(8,128)S(1)}, u32[]{:S(2)}, u32[]{:S(2)}) collective-permute-start(f32[16,66,1]{1,0,2:T(8,128)S(1)} %get-tuple-element.24), channel_id=1, source_target_pairs={{1,0},{2,1},{3,2},{4,3},{5,4},{6,5},{7,6},{9,8},{10,9},{11,10},{12... | collective-permute-start | bytes 12680 | tf_op jit(solution)/shard_map/ppermute | solution.py:19
  147.5 14.8 %copy-start.9 = (f32[64,128]{0,1:T(8,128)S(1)}, f32[64,128]{0,1:T(8,128)}, u32[]{:S(2)}) copy-start(f32[64,128]{0,1:T(8,128)} %copy-done.8) | copy-start | bytes 98308
  147.5 14.8 %copy-start.11 = (f32[64,128]{0,1:T(8,128)S(1)}, f32[64,128]{0,1:T(8,128)}, u32[]{:S(2)}) copy-start(f32[64,128]{0,1:T(8,128)} %copy-done.10) | copy-start | bytes 98308
  147.5 14.8 %copy-start.13 = (f32[64,128]{0,1:T(8,128)S(1)}, f32[64,128]{0,1:T(8,128)}, u32[]{:S(2)}) copy-start(f32[64,128]{0,1:T(8,128)} %copy-done.12) | copy-start | bytes 98308
  147.6 14.8 %collective-permute-start.15 = (f32[16,66,1]{1,0,2:T(8,128)S(1)}, f32[16,66,1]{1,0,2:T(8,128)S(1)}, u32[]{:S(2)}, u32[]{:S(2)}) collective-permute-start(f32[16,66,1]{1,0,2:T(8,128)S(1)} %get-tuple-element.25), channel_id=1, source_target_pairs={{0,1},{1,2},{2,3},{3,4},{4,5},{5,6},{6,7},{8,9},{9,10},{10,11},{11... | collective-permute-start | bytes 12680 | tf_op jit(solution)/shard_map/ppermute | solution.py:18
  167.5 31.3 %collective-permute-start.19 = (f32[16,1,128]{2,0,1:T(8,128)S(1)}, f32[16,1,128]{2,0,1:T(8,128)S(1)}, u32[]{:S(2)}, u32[]{:S(2)}) collective-permute-start(f32[16,1,128]{2,0,1:T(8,128)S(1)} %copy.91), channel_id=1, source_target_pairs={{8,0},{16,8},{24,16},{32,24},{40,32},{48,40},{56,48},{64,56},{72,6... | collective-permute-start | bytes 24584 | tf_op jit(solution)/shard_map/ppermute | solution.py:19
  180.7 17.6 %collective-permute-start.17 = (f32[16,1,128]{2,0,1:T(8,128)S(1)}, f32[16,1,128]{2,0,1:T(8,128)S(1)}, u32[]{:S(2)}, u32[]{:S(2)}) collective-permute-start(f32[16,1,128]{2,0,1:T(8,128)S(1)} %copy.88), channel_id=1, source_target_pairs={{0,8},{8,16},{16,24},{24,32},{32,40},{40,48},{48,56},{56,64},{64,7... | collective-permute-start | bytes 24584 | tf_op jit(solution)/shard_map/ppermute | solution.py:18
  183.5 32.8 %collective-permute-start.20 = (f32[6,66,1]{2,1,0:T(8,128)}, f32[6,66,1]{2,1,0:T(8,128)S(1)}, u32[]{:S(2)}, u32[]{:S(2)}) collective-permute-start(f32[6,66,1]{2,1,0:T(8,128)} %get-tuple-element.48), channel_id=1, source_target_pairs={{0,1},{1,2},{2,3},{3,4},{4,5},{5,6},{6,7},{8,9},{9,10},{10,11},{11... | collective-permute-start | bytes 4760 | tf_op jit(solution)/shard_map/ppermute | solution.py:18
  197.0 22.2 %collective-permute-start.22 = (f32[6,66,1]{2,1,0:T(8,128)}, f32[6,66,1]{2,1,0:T(8,128)}, u32[]{:S(2)}, u32[]{:S(2)}) collective-permute-start(f32[6,66,1]{2,1,0:T(8,128)} %get-tuple-element.49), channel_id=1, source_target_pairs={{1,0},{2,1},{3,2},{4,3},{5,4},{6,5},{7,6},{9,8},{10,9},{11,10},{12... | collective-permute-start | bytes 4760 | tf_op jit(solution)/shard_map/ppermute | solution.py:19
  199.4 19.8 %copy-start.16 = (f32[6,64,128]{2,1,0:T(8,128)S(1)}, f32[6,64,128]{2,1,0:T(8,128)}, u32[]{:S(2)}) copy-start(f32[6,64,128]{2,1,0:T(8,128)} %broadcast_dynamic-update-slice_fusion) | copy-start | bytes 589828
  200.4 20.1 %collective-permute-start.21 = (f32[16,66,1]{1,0,2:T(8,128)S(1)}, f32[16,66,1]{1,0,2:T(8,128)S(1)}, u32[]{:S(2)}, u32[]{:S(2)}) collective-permute-start(f32[16,66,1]{1,0,2:T(8,128)S(1)} %get-tuple-element.22), channel_id=1, source_target_pairs={{0,1},{1,2},{2,3},{3,4},{4,5},{5,6},{6,7},{8,9},{9,10},{10,11},{11... | collective-permute-start | bytes 12680 | tf_op jit(solution)/shard_map/ppermute | solution.py:18
  215.0 14.0 %collective-permute-start.23 = (f32[16,66,1]{1,0,2:T(8,128)S(1)}, f32[16,66,1]{1,0,2:T(8,128)S(1)}, u32[]{:S(2)}, u32[]{:S(2)}) collective-permute-start(f32[16,66,1]{1,0,2:T(8,128)S(1)} %get-tuple-element.23), channel_id=1, source_target_pairs={{1,0},{2,1},{3,2},{4,3},{5,4},{6,5},{7,6},{9,8},{10,9},{11,10},{12... | collective-permute-start | bytes 12680 | tf_op jit(solution)/shard_map/ppermute | solution.py:19
  233.8 6.7 %collective-permute-start.24 = (f32[16,1,128]{2,0,1:T(8,128)S(1)}, f32[16,1,128]{2,0,1:T(8,128)S(1)}, u32[]{:S(2)}, u32[]{:S(2)}) collective-permute-start(f32[16,1,128]{2,0,1:T(8,128)S(1)} %copy.97), channel_id=1, source_target_pairs={{0,8},{8,16},{16,24},{24,32},{32,40},{40,48},{48,56},{56,64},{64,7... | collective-permute-start | bytes 24584 | tf_op jit(solution)/shard_map/ppermute | solution.py:18
  236.4 5.0 collective-permute-start.25
  242.9 14.5 %collective-permute-start.26 = (f32[16,66,1]{1,0,2:T(8,128)S(1)}, f32[16,66,1]{1,0,2:T(8,128)S(1)}, u32[]{:S(2)}, u32[]{:S(2)}) collective-permute-start(f32[16,66,1]{1,0,2:T(8,128)S(1)} %get-tuple-element.20), channel_id=1, source_target_pairs={{0,1},{1,2},{2,3},{3,4},{4,5},{5,6},{6,7},{8,9},{9,10},{10,11},{11... | collective-permute-start | bytes 12680 | tf_op jit(solution)/shard_map/ppermute | solution.py:18
  256.1 13.1 %collective-permute-start.27 = (f32[16,66,1]{1,0,2:T(8,128)S(1)}, f32[16,66,1]{1,0,2:T(8,128)S(1)}, u32[]{:S(2)}, u32[]{:S(2)}) collective-permute-start(f32[16,66,1]{1,0,2:T(8,128)S(1)} %get-tuple-element.21), channel_id=1, source_target_pairs={{1,0},{2,1},{3,2},{4,3},{5,4},{6,5},{7,6},{9,8},{10,9},{11,10},{12... | collective-permute-start | bytes 12680 | tf_op jit(solution)/shard_map/ppermute | solution.py:19
  274.1 16.7 %collective-permute-start.28 = (f32[16,1,128]{2,0,1:T(8,128)S(1)}, f32[16,1,128]{2,0,1:T(8,128)S(1)}, u32[]{:S(2)}, u32[]{:S(2)}) collective-permute-start(f32[16,1,128]{2,0,1:T(8,128)S(1)} %copy.103), channel_id=1, source_target_pairs={{0,8},{8,16},{16,24},{24,32},{32,40},{40,48},{48,56},{56,64},{64,7... | collective-permute-start | bytes 24584 | tf_op jit(solution)/shard_map/ppermute | solution.py:18
  277.6 13.9 %collective-permute-start.29 = (f32[16,1,128]{2,0,1:T(8,128)S(1)}, f32[16,1,128]{2,0,1:T(8,128)S(1)}, u32[]{:S(2)}, u32[]{:S(2)}) collective-permute-start(f32[16,1,128]{2,0,1:T(8,128)S(1)} %copy.105), channel_id=1, source_target_pairs={{8,0},{16,8},{24,16},{32,24},{40,32},{48,40},{56,48},{64,56},{72,6... | collective-permute-start | bytes 24584 | tf_op jit(solution)/shard_map/ppermute | solution.py:19
  293.1 13.2 %collective-permute-start.30 = (f32[16,66,1]{1,0,2:T(8,128)S(1)}, f32[16,66,1]{1,0,2:T(8,128)S(1)}, u32[]{:S(2)}, u32[]{:S(2)}) collective-permute-start(f32[16,66,1]{1,0,2:T(8,128)S(1)} %get-tuple-element.18), channel_id=1, source_target_pairs={{0,1},{1,2},{2,3},{3,4},{4,5},{5,6},{6,7},{8,9},{9,10},{10,11},{11... | collective-permute-start | bytes 12680 | tf_op jit(solution)/shard_map/ppermute | solution.py:18
  305.0 13.4 %collective-permute-start.31 = (f32[16,66,1]{1,0,2:T(8,128)S(1)}, f32[16,66,1]{1,0,2:T(8,128)S(1)}, u32[]{:S(2)}, u32[]{:S(2)}) collective-permute-start(f32[16,66,1]{1,0,2:T(8,128)S(1)} %get-tuple-element.19), channel_id=1, source_target_pairs={{1,0},{2,1},{3,2},{4,3},{5,4},{6,5},{7,6},{9,8},{10,9},{11,10},{12... | collective-permute-start | bytes 12680 | tf_op jit(solution)/shard_map/ppermute | solution.py:19
  323.2 16.4 %collective-permute-start.32 = (f32[16,1,128]{2,0,1:T(8,128)S(1)}, f32[16,1,128]{2,0,1:T(8,128)S(1)}, u32[]{:S(2)}, u32[]{:S(2)}) collective-permute-start(f32[16,1,128]{2,0,1:T(8,128)S(1)} %copy.109), channel_id=1, source_target_pairs={{0,8},{8,16},{16,24},{24,32},{32,40},{40,48},{48,56},{56,64},{64,7... | collective-permute-start | bytes 24584 | tf_op jit(solution)/shard_map/ppermute | solution.py:18
  325.6 14.8 %collective-permute-start.33 = (f32[16,1,128]{2,0,1:T(8,128)S(1)}, f32[16,1,128]{2,0,1:T(8,128)S(1)}, u32[]{:S(2)}, u32[]{:S(2)}) collective-permute-start(f32[16,1,128]{2,0,1:T(8,128)S(1)} %copy.111), channel_id=1, source_target_pairs={{8,0},{16,8},{24,16},{32,24},{40,32},{48,40},{56,48},{64,56},{72,6... | collective-permute-start | bytes 24584 | tf_op jit(solution)/shard_map/ppermute | solution.py:19
  342.0 14.8 %collective-permute-start.34 = (f32[16,66,1]{1,0,2:T(8,128)S(1)}, f32[16,66,1]{1,0,2:T(8,128)S(1)}, u32[]{:S(2)}, u32[]{:S(2)}) collective-permute-start(f32[16,66,1]{1,0,2:T(8,128)S(1)} %get-tuple-element.16), channel_id=1, source_target_pairs={{0,1},{1,2},{2,3},{3,4},{4,5},{5,6},{6,7},{8,9},{9,10},{10,11},{11... | collective-permute-start | bytes 12680 | tf_op jit(solution)/shard_map/ppermute | solution.py:18
  355.2 13.1 %collective-permute-start.35 = (f32[16,66,1]{1,0,2:T(8,128)S(1)}, f32[16,66,1]{1,0,2:T(8,128)S(1)}, u32[]{:S(2)}, u32[]{:S(2)}) collective-permute-start(f32[16,66,1]{1,0,2:T(8,128)S(1)} %get-tuple-element.17), channel_id=1, source_target_pairs={{1,0},{2,1},{3,2},{4,3},{5,4},{6,5},{7,6},{9,8},{10,9},{11,10},{12... | collective-permute-start | bytes 12680 | tf_op jit(solution)/shard_map/ppermute | solution.py:19
  (13 other events, 36.6 us)
where the time goes:
time: 507 us; the launch traced here: 498 us
  starting transfers between devices  246 us (49%)
  blocking collectives  117 us (23%)
  waiting for transfers between devices  55.5 us (11%)
  other arithmetic  38.9 us (8%)
  local copies, waits for them, and re-layouts  36.2 us (7%)
    ppermute x18, starting transfers between devices, extended(): before = lax.ppermute(last, axis, up)  138 us
    psum x1, blocking collectives, per_device(): gram = lax.psum(local_gram, ('gx', 'gy'))  117 us
    ppermute x18, starting transfers between devices, extended(): after = lax.ppermute(leading, axis, down)  108 us
    ppermute x18, waiting for transfers between devices, extended(): after = lax.ppermute(leading, axis, down)  47.7 us
    add x4, other arithmetic, adjoint_step(): coefs[0, 1:-1, 1:-1] * padded[:, 1:-1, 1:-1]  16.2 us
    unnamed x58, local copies, waits for them, and re-layouts  14.8 us
    add x3, other arithmetic, forward_step(): coefs[0] * padded[:, 1:-1, 1:-1] + coefs[1] * padded[:, 2:, 1:-1]  11.8 us
  transfers between devices with their start and end apart: 36, of which 13 were waited for; matrix products, arithmetic and copies ran while one was open for 3% of the time, Pallas kernels for 0%

commit v1 on v0

v1 whole, which is shorter than its diff:
```python
import functools
import math

import jax
import jax.numpy as jnp
from jax import lax
from jax.experimental import pallas as pl
from jax.experimental.pallas import tpu as pltpu
from jax.sharding import PartitionSpec as P

R = 16
STEPS = 4
D = 2 * STEPS
ROWS, COLS = 64, 128
TOP = 16
BOT = TOP + ROWS
FRAME = 96
MESH = pl.DeviceIdType.MESH


def lanes(rows=8):
    return lax.broadcasted_iota(jnp.int32, (rows, COLS), 1)


def roll(x, shift):
    shift = shift % COLS
    return x if shift == 0 else pltpu.roll(x, shift, axis=x.ndim - 1)


def pick(index, parts):
    out = parts[0]
    for r in range(1, len(parts)):
        out = jnp.where(index == r, parts[r], out)
    return out


def coefficients(ea, no, di):
    e = di + jnp.maximum(-ea, 0.0)
    w = di + jnp.maximum(ea, 0.0)
    n = di + jnp.maximum(-no, 0.0)
    s = di + jnp.maximum(no, 0.0)
    return 1.0 - e - w - n - s, e, w, n, s


def stencil(k, v, co, prec, src, dst, items):
    at = v * 8
    mid, up, down = pl.ds(at, 8), pl.ds(at - 1, 8), pl.ds(at + 1, 8)
    c, n, s = co(0, mid), co(3, mid), co(4, mid)
    if k <= STEPS:
        e, w = co(1, mid), co(2, mid)
    else:
        e, w = co(1, up), co(2, down)
    p = prec(mid) if k == STEPS else None
    for d in items:
        f = src(d, mid)
        if k <= STEPS:
            out = c * f + e * src(d, down) + w * src(d, up) + n * roll(f, -1) + s * roll(f, 1)
            if k == STEPS:
                out = p * out
        else:
            out = c * f + e * src(d, up) + w * src(d, down) + roll(n * f, 1) + roll(s * f, -1)
        dst(d, mid, out)


def kernel(dims, d_hbm, ea_hbm, no_hbm, di_hbm, pr_hbm, basis, factor, fd, prm, co, hx, hp, st, sp, sc, ws, wr, ds_, dr, acc,
           gs, g1, g2, cb, ob, in_sem, xs, xr, ps, pr, ys, yr, dgs, dgr, gsend, grecv, osem):
    nx, nzl, nc, ny, nzh = dims
    ngx, ngy = nx * nzl * nc, ny * nzh
    gx, gy = lax.axis_index("gx"), lax.axis_index("gy")
    ix, izl, ic = gx // (nzl * nc), (gx // nc) % nzl, gx % nc
    iy, izh = gy // nzh, gy % nzh
    has = (gy > 0, gy < ngy - 1)
    xm, xp = (gx + ngx - 1) % ngx, (gx + 1) % ngx
    xdev = (xm, xp)
    ydev = (jnp.maximum(gy - 1, 0), jnp.minimum(gy + 1, ngy - 1))

    i1, n1 = (ic * nx + ix) * ny + iy, nc * nx * ny
    i2, n2 = izh * nzl + izl, nzh * nzl

    def member1(j):
        v = (i1 + j) % n1
        c, x, y = v // (nx * ny), (v // ny) % nx, v % ny
        return {"gx": (x * nzl + izl) * nc + c, "gy": y * nzh + izh}

    def member2(j):
        v = (i2 + j) % n2
        return {"gx": (ix * nzl + v % nzl) * nc + ic, "gy": iy * nzh + v // nzl}

    barrier = pltpu.get_barrier_semaphore()

    def hello(dev):
        pl.semaphore_signal(barrier, inc=1, device_id=dev, device_id_type=MESH)

    for s in range(2):
        @pl.when(has[s])
        def _():
            hello({"gx": gx, "gy": ydev[s]})
            for t in range(2):
                hello({"gx": xdev[t], "gy": ydev[s]})
    for t in range(2):
        hello({"gx": xdev[t], "gy": gy})

    loads = [pltpu.make_async_copy(d_hbm, fd.at[0, :, pl.ds(TOP, ROWS), :], in_sem.at[0])]
    for a, ref in enumerate((ea_hbm, no_hbm, di_hbm, pr_hbm)):
        loads.append(pltpu.make_async_copy(ref, prm.at[a, pl.ds(TOP, ROWS), :], in_sem.at[a + 1]))
    for c in loads:
        c.start()
    for j in range(n2 // 2, n2):
        hello(member2(j))
    for j in range(1, n2 // 2):
        hello(member2(j))
    for j in range(1, n1):
        hello(member1(j))
    for s in range(2):
        @pl.when(jnp.logical_not(has[s]))
        def _():
            wr[s] = jnp.zeros((80, COLS), jnp.float32)
            for t in range(2):
                dr[s, t] = jnp.zeros((16, COLS), jnp.float32)
    for c in loads:
        c.wait()

    lane = lanes()
    blk = (lane // 32, ((lane + 16) % COLS) // 32)
    halo = (lane % 32 < 8, (lane % 32 >= 8) & (lane % 32 < 16))

    def tile(v):
        return pl.ds(pl.multiple_of(v * 8, 8), 8) if not isinstance(v, int) else pl.ds(v * 8, 8)

    def pack_fields(v):
        for q in range(4):
            rolled = [roll(fd[0, q + 4 * r, tile(v), :], 8 + 32 * r) for r in range(4)]
            for s in range(2):
                st[0, 4 * s + q, tile(v), :] = pick(blk[s], rolled)

    def pack_params(v):
        for a in range(4):
            rolled = [roll(prm[a, tile(v), :], 8 + 32 * r) for r in range(4)]
            for s in range(2):
                sp[s, a, tile(v), :] = pick(blk[s], rolled)

    def main_coefs(v):
        for a, x in enumerate(coefficients(*(prm[b, tile(v), :] for b in range(3)))):
            co[a, tile(v), :] = x

    eighth = (lane % 32) // 8
    for v in range(TOP // 8, BOT // 8):
        pack_fields(v)
        w = pl.ds(v * 8 - TOP, 8)
        for s in range(2):
            ws[s, w, :] = pick(eighth, [roll(st[0, 4 * s + q, tile(v), :], 8 * q - 8 + 8 * s) for q in range(4)])
    wide = [[], []]
    for v in range(TOP // 8, BOT // 8):
        for s in range(2):
            wide[s].append(pick(lane // 8, [roll(prm[a, tile(v), :], 8 * a + 8 * s) for a in range(4)]))
    for s in range(2):
        for h in range(2):
            ws[s, pl.ds(ROWS + 8 * h, 8), :] = pick(lane // 32, [roll(wide[s][2 * g + h], 32 * g) for g in range(4)])
        for t in range(2):
            ds_[s, t, pl.ds(0, 8), :] = ws[s, pl.ds(56 * t, 8), :]
            ds_[s, t, pl.ds(8, 8), :] = wide[s][7 * t]

    partners = 2 + 3 * (has[0].astype(jnp.int32) + has[1].astype(jnp.int32)) + (n1 - 1) + (n2 - 1)
    pl.semaphore_wait(barrier, partners)

    def remote(src, dst, s_sem, r_sem, dev):
        return pltpu.make_async_remote_copy(src_ref=src, dst_ref=dst, send_sem=s_sem, recv_sem=r_sem, device_id=dev,
                                            device_id_type=MESH)

    def ycopies(s):
        dev = {"gx": gx, "gy": ydev[s]}
        return [remote(ws.at[s], wr.at[1 - s], ys.at[s], yr.at[1 - s], dev)] + [
            remote(ds_.at[s, t], dr.at[1 - s, 1 - t], dgs.at[s, t], dgr.at[1 - s, 1 - t], {"gx": xdev[t], "gy": ydev[s]})
            for t in range(2)
        ]

    def xcopies(t):
        dev = {"gx": xdev[t], "gy": gy}
        rows = pl.ds(TOP + 56 * t, 8)
        return [remote(fd.at[0, :, rows, :], hx.at[1 - t], xs.at[t], xr.at[1 - t], dev),
                remote(prm.at[:, rows, :], hp.at[1 - t], ps.at[t], pr.at[1 - t], dev)]

    for s in range(2):
        @pl.when(has[s])
        def _():
            for c in ycopies(s):
                c.start()
    for t in range(2):
        for c in xcopies(t):
            c.start()

    for v in range(TOP // 8, BOT // 8):
        main_coefs(v)
        pack_params(v)

    def main_step(k, v, items):
        def put(d, rows, x):
            fd[k, d, rows, :] = x
        stencil(k, v, lambda a, rows: co[a, rows, :], lambda rows: prm[3, rows, :], lambda d, rows: fd[k - 1, d, rows, :],
                put, items)

    for k in range(1, D + 1):
        def some(g, _):
            for v in range(TOP // 8, BOT // 8):
                main_step(k, v, [4 * g + i for i in range(4)])
            return 0
        lax.fori_loop(0, R // 4, some, 0)

    for t in range(2):
        for c in xcopies(t):
            c.wait_recv()
    edge = (TOP // 8 - 1, BOT // 8)
    for t in range(2):
        rows = tile(edge[t])
        for d in range(R):
            fd[0, d, rows, :] = hx[t, d]
        for a in range(4):
            prm[a, rows, :] = hp[t, a]
        main_coefs(edge[t])
        pack_params(edge[t])
        pack_fields(edge[t])
    for k in range(1, D + 1):
        for v in (1, 2, 9, 10) if k < D else (2, 9):
            main_step(k, v, range(R))

    for s in range(2):
        @pl.when(has[s])
        def _():
            for c in ycopies(1 - s):
                c.wait_recv()
    for s in range(2):
        for v in range(1, 11):
            if v in edge:
                t = edge.index(v)
                x = dr[s, t, pl.ds(0, 8), :]
            else:
                x = wr[s, pl.ds(v * 8 - TOP, 8), :]
            for q in range(4):
                st[0, 4 * s + q, tile(v), :] = jnp.where(halo[s], roll(x, 8 * s - 8 * q), st[0, 4 * s + q, tile(v), :])
            if v in edge:
                y = dr[s, t, pl.ds(8, 8), :]
            else:
                g, h = divmod(v - 2, 2)
                y = roll(wr[s, pl.ds(ROWS + 8 * h, 8), :], -32 * g)
            y = jnp.where(lane < 32, y, 0.0)
            y = y + roll(y, 32)
            y = y + roll(y, 64)
            par = [jnp.where(halo[s], roll(y, 8 * s - 8 * a), sp[s, a, tile(v), :]) for a in range(4)]
            outside = halo[s] & jnp.logical_not(has[s])
            for a, x in enumerate(coefficients(*par[:3])):
                sc[s, a, tile(v), :] = jnp.where(outside, 0.0, x)
            sc[s, 5, tile(v), :] = par[3]
    for k in range(1, D + 1):
        def put(d, rows, x):
            st[k % 2, d, rows, :] = x
        for v in range(1, 11) if k < D else range(2, 10):
            for s in range(2):
                stencil(k, v, lambda a, rows: sc[s, a, rows, :], lambda rows: sc[s, 5, rows, :],
                        lambda d, rows: st[(k - 1) % 2, d, rows, :], put, range(4 * s, 4 * s + 4))
    rim = (lane < 8) | (lane >= COLS - 8)
    for v in range(TOP // 8, BOT // 8):
        for q in range(4):
            both = jnp.where(lane % 32 >= 8, st[0, q, tile(v), :], st[0, 4 + q, tile(v), :])
            for r in range(4):
                d = q + 4 * r
                fd[D, d, tile(v), :] = jnp.where(rim, roll(both, -32 * r - 8), fd[D, d, tile(v), :])

    for bi in range(4):
        for bj in range(bi + 1):
            sums = {}
            for v in range(TOP // 8, BOT // 8):
                left = [fd[D, 4 * bi + i, tile(v), :] for i in range(4)]
                right = left if bi == bj else [fd[D, 4 * bj + j, tile(v), :] for j in range(4)]
                for i in range(4):
                    for j in range(4):
                        if bi > bj or i >= j:
                            x = left[i] * right[j]
                            sums[i, j] = sums[i, j] + x if (i, j) in sums else x
            for (i, j), x in sums.items():
                i, j = 4 * bi + i, 4 * bj + j
                acc[16 * i + j] = x
                if i != j:
                    acc[16 * j + i] = x
    sub = lax.broadcasted_iota(jnp.int32, (8, COLS), 0)
    rows = []
    for g in range(32):
        now = [acc[8 * g + i] for i in range(8)]
        for width in (4, 2, 1):
            low = sub % (2 * width) < width
            now = [jnp.where(low, now[i], now[i + width]) + pltpu.roll(jnp.where(low, now[i + width], now[i]), width, axis=0)
                   if width == 4 else
                   jnp.where(low, now[i], now[i + width])
                   + jnp.where(low, pltpu.roll(now[i], 8 - width, axis=0), pltpu.roll(now[i + width], width, axis=0))
                   for i in range(width)]
        rows.append(now[0])
    stacked = jnp.concatenate(rows, axis=0)
    total = lax.dot_general(jnp.ones((8, COLS), jnp.float32), stacked, (((1,), (1,)), ((), ())),
                            precision=lax.Precision.HIGHEST, preferred_element_type=jnp.float32)

    def spread(value, h, n, index, member, slots, which):
        for i in range(2):
            gs[which, pl.ds(i, 1), :] = value[i]
        slots[index] = gs[which]
        copies = [remote(gs.at[which], slots.at[index], gsend.at[which], grecv.at[which], member(j)) for j in range(1, n)]
        for c in copies:
            c.start()
        some = slots.at[pl.ds(0, n - 1)]
        pltpu.make_async_copy(some, some, grecv.at[which]).wait()
        parts = [slots[j] for j in range(n)]
        while len(parts) > 1:
            parts = [parts[j] + parts[j + 1] if j + 1 < len(parts) else parts[j] for j in range(0, len(parts), 2)]
        return parts[0]

    mine = [total[0:1, 0:COLS], total[0:1, COLS:2 * COLS]]
    one = spread(mine, 0, n1, i1, member1, g1, 0)
    two = spread([one[0:1], one[1:2]], 0, n2, i2, member2, g2, 1)

    halves = []
    for h in range(2):
        wide_row = jnp.broadcast_to(two[h:h + 1], (8, COLS))
        halves.append(pick(sub, [roll(wide_row, -16 * i) for i in range(8)]))
    m = jnp.concatenate(halves, axis=0)
    lane16, row16 = lanes(R), lax.broadcasted_iota(jnp.int32, (R, COLS), 0)
    m = jnp.where(lane16 < R, m, jnp.where(lane16 - R == row16, 1.0, 0.0))
    pivots = jnp.ones((R, COLS), jnp.float32)
    for k in range(R):
        row = m[k:k + 1, :]
        pivot = jnp.broadcast_to(m[k:k + 1, k:k + 1], (1, COLS))
        pivots = jnp.where(row16 == k, pivot, pivots)
        if k < R - 1:
            times = jnp.where(row16 > k, jnp.broadcast_to(m[:, k:k + 1], (R, COLS)) / pivot, 0.0)
            m = m - times * row
    m = m / jnp.sqrt(pivots)
    scale = math.sqrt(float(ROWS * COLS * ngx * ngy))
    factor[...] = (jnp.where(lane16 >= row16, m, 0.0) * (1.0 / scale))[:, :R]
    m = m * scale
    for j in range(R):
        cb[j] = jnp.broadcast_to(m[:, R + j:R + j + 1], (R, COLS))
    outs = []
    for b in range(4):
        sums = {}
        for j in range(4 * b + 4):
            src = [fd[D, j, tile(v), :] for v in range(2, 10)]
            for i in range(max(j, 4 * b), 4 * b + 4):
                weight = jnp.broadcast_to(cb[j, i:i + 1, :], (8, COLS))
                for v in range(8):
                    x = weight * src[v]
                    sums[i, v] = sums[i, v] + x if (i, v) in sums else x
        for (i, v), x in sums.items():
            ob[i, pl.ds(8 * v, 8), :] = x
        outs.append(pltpu.make_async_copy(ob.at[pl.ds(4 * b, 4)], basis.at[pl.ds(4 * b, 4)], osem.at[b]))
        outs[-1].start()

    for s in range(2):
        @pl.when(has[s])
        def _():
            for c in ycopies(s):
                c.wait_send()
    for t in range(2):
        for c in xcopies(t):
            c.wait_send()
    for which, n, slots in ((0, n1, g1), (1, n2, g2)):
        some = slots.at[pl.ds(0, n - 1)]
        pltpu.make_async_copy(some, some, gsend.at[which]).wait()
    for c in outs:
        c.wait()


def build(mesh, dims):
    nx, nzl, nc, ny, nzh = dims
    f32 = jnp.float32
    vmem = lambda *shape: pltpu.VMEM(shape, f32)
    dma = lambda *shape: pltpu.SemaphoreType.DMA(shape)
    call = pl.pallas_call(
        functools.partial(kernel, dims),
        name="sketch",
        out_shape=(jax.ShapeDtypeStruct((R, ROWS, COLS), f32), jax.ShapeDtypeStruct((R, R), f32)),
        in_specs=[pl.BlockSpec(memory_space=pl.ANY)] * 5,
        out_specs=(pl.BlockSpec(memory_space=pl.ANY), pl.BlockSpec(memory_space=pltpu.VMEM)),
        scratch_shapes=[
            vmem(D + 1, R, FRAME, COLS), vmem(4, FRAME, COLS), vmem(5, FRAME, COLS),
            vmem(2, R, 8, COLS), vmem(2, 4, 8, COLS),
            vmem(2, 8, FRAME, COLS), vmem(2, 4, FRAME, COLS), vmem(2, 6, FRAME, COLS),
            vmem(2, 80, COLS), vmem(2, 80, COLS), vmem(2, 2, 16, COLS), vmem(2, 2, 16, COLS),
            vmem(R * R, 8, COLS), vmem(2, 2, COLS), vmem(nc * nx * ny, 2, COLS), vmem(nzh * nzl, 2, COLS),
            vmem(R, R, COLS), vmem(R, ROWS, COLS),
            dma(5), dma(2), dma(2), dma(2), dma(2), dma(2), dma(2), dma(2, 2), dma(2, 2), dma(2), dma(2), dma(4),
        ],
        compiler_params=pltpu.CompilerParams(collective_id=0, has_side_effects=True, vmem_limit_bytes=48 * 2**20),
    )
    return jax.shard_map(
        call,
        mesh=mesh,
        in_specs=(P(None, "gx", "gy"),) + (P("gx", "gy"),) * 4,
        out_specs=(P(None, "gx", "gy"), P()),
        check_vma=False,
    )


def solution(mesh):
    return build(mesh, (mesh.shape["gx"] // 16, 8, 2, mesh.shape["gy"] // 2, 2))
```

time: 507 us -> 59 us (0.12); the launches traced: 498 us -> 58.6 us
  starting transfers between devices: 246 us -> 0 us
  blocking collectives: 117 us -> 0 us
  waiting for transfers between devices: 55.5 us -> 0 us
  Pallas kernels: 0 us -> 52.4 us
  other arithmetic: 38.9 us -> 0 us
  local copies, waits for them, and re-layouts: 36.2 us -> 5.46 us
    ppermute x36 -> x0, starting transfers between devices: 246 us -> none  [the longest x18 138 us: extended(): before = lax.ppermute(last, axis, up)]
    psum x1 -> x0, blocking collectives: 117 us -> none  [per_device(): gram = lax.psum(local_gram, ('gx', 'gy'))]
    ppermute x36 -> x0, waiting for transfers between devices: 55.5 us -> none  [the longest x18 47.7 us: extended(): after = lax.ppermute(leading, axis, down)]
    pallas_call x0 -> x1, Pallas kernels: none -> 52.4 us
    add x7 -> x0, other arithmetic: 28 us -> none  [the longest x4 16.2 us: adjoint_step(): coefs[0, 1:-1, 1:-1] * padded[:, 1:-1, 1:-1]]
    slice x24 -> x0, local copies, waits for them, and re-layouts: 11.1 us -> none  [the longest x17 7.98 us: extended(): last = lax.slice_in_dim(value, length - width, length, axis=dim)]
    unnamed x58 -> x12, local copies, waits for them, and re-layouts: 14.8 us -> 5.46 us
    ppermute x16 -> x0, local copies, waits for them, and re-layouts: 8.39 us -> none  [the longest x8 4.19 us: extended(): before = lax.ppermute(last, axis, up)]
  transfers between devices with their start and end apart: 36 -> 0, of which waited for: 13 -> 0; matrix products, arithmetic and copies ran while one was open for 3% -> 0% of each run, Pallas kernels for 0% -> 0%
where the time goes in v1:
time: 59 us; the launch traced here: 58.6 us
  Pallas kernels  52.4 us (89%)
  local copies, waits for them, and re-layouts  5.46 us (9%)
  between operations  0.65 us (1%)
    pallas_call x1, Pallas kernels  52.4 us
    unnamed x12, local copies, waits for them, and re-layouts  5.46 us

profile of v1, /device:TPU:1, one launch (start us, length us, event | category | flops | bytes accessed | tf_op | source)
XLA Modules:
  0.0 58.6 jit_solution(9015598410094668289)
XLA Ops:
  0.6 0.0 copy-start
  0.6 1.0 %copy-done = f32[16,64,128]{2,1,0:T(8,128)S(1)} copy-done((f32[16,64,128]{2,1,0:T(8,128)S(1)}, f32[16,64,128]{2,1,0:T(8,128)}, u32[]{:S(2)}) %copy-start) | copy-done | bytes 524312
  1.7 0.0 copy-start.1
  1.7 0.8 %copy-done.1 = f32[64,128]{1,0:T(8,128)S(1)} copy-done((f32[64,128]{1,0:T(8,128)S(1)}, f32[64,128]{1,0:T(8,128)}, u32[]{:S(2)}) %copy-start.1) | copy-done | bytes 32792
  2.4 0.0 copy-start.2
  2.4 0.8 %copy-done.2 = f32[64,128]{1,0:T(8,128)S(1)} copy-done((f32[64,128]{1,0:T(8,128)S(1)}, f32[64,128]{1,0:T(8,128)}, u32[]{:S(2)}) %copy-start.2) | copy-done | bytes 32792
  3.2 0.0 copy-start.3
  3.2 0.8 %copy-done.3 = f32[64,128]{1,0:T(8,128)S(1)} copy-done((f32[64,128]{1,0:T(8,128)S(1)}, f32[64,128]{1,0:T(8,128)}, u32[]{:S(2)}) %copy-start.3) | copy-done | bytes 32792
  3.9 0.0 copy-start.4
  4.0 0.8 %copy-done.4 = f32[64,128]{1,0:T(8,128)S(1)} copy-done((f32[64,128]{1,0:T(8,128)S(1)}, f32[64,128]{1,0:T(8,128)}, u32[]{:S(2)}) %copy-start.4) | copy-done | bytes 32792
  4.7 52.4 %sketch.1 = (f32[16,64,128]{2,1,0:T(8,128)S(1)}, f32[16,16]{1,0:T(8,128)S(1)}) custom-call(f32[16,64,128]{2,1,0:T(8,128)S(1)} %copy-done, f32[64,128]{1,0:T(8,128)S(1)} %copy-done.1, f32[64,128]{1,0:T(8,128)S(1)} %copy-done.2, f32[64,128]{1,0:T(8,128)S(1)} %copy-done.3, f32[64,128]{1,0:T(8,128)S(1)} %copy-done.4), custom_call_target="tpu_custom_call" | custom-call | tf_op jit(solution)/shard_map/sketch/pallas_call
  57.2 0.8 %copy.9 = f32[16,64,128]{2,1,0:T(8,128)} copy(f32[16,64,128]{2,1,0:T(8,128)S(1)} %get-tuple-element.4) | data formatting | bytes 1048576
  58.0 0.6 %copy.10 = f32[16,16]{1,0:T(8,128)} copy(f32[16,16]{1,0:T(8,128)S(1)} %get-tuple-element.5) | data formatting | bytes 2048
Async XLA Ops:
  0.6 1.0 %copy-start = (f32[16,64,128]{2,1,0:T(8,128)S(1)}, f32[16,64,128]{2,1,0:T(8,128)}, u32[]{:S(2)}) copy-start(f32[16,64,128]{2,1,0:T(8,128)} %d_hbm.1) | copy-start | bytes 1572868
  1.7 0.8 %copy-start.1 = (f32[64,128]{1,0:T(8,128)S(1)}, f32[64,128]{1,0:T(8,128)}, u32[]{:S(2)}) copy-start(f32[64,128]{1,0:T(8,128)} %ea_hbm.1) | copy-start | bytes 98308
  2.4 0.8 %copy-start.2 = (f32[64,128]{1,0:T(8,128)S(1)}, f32[64,128]{1,0:T(8,128)}, u32[]{:S(2)}) copy-start(f32[64,128]{1,0:T(8,128)} %no_hbm.1) | copy-start | bytes 98308
  3.2 0.8 %copy-start.3 = (f32[64,128]{1,0:T(8,128)S(1)}, f32[64,128]{1,0:T(8,128)}, u32[]{:S(2)}) copy-start(f32[64,128]{1,0:T(8,128)} %di_hbm.1) | copy-start | bytes 98308
  3.9 0.8 %copy-start.4 = (f32[64,128]{1,0:T(8,128)S(1)}, f32[64,128]{1,0:T(8,128)}, u32[]{:S(2)}) copy-start(f32[64,128]{1,0:T(8,128)} %pr_hbm.1) | copy-start | bytes 98308

commit v2 on v1

v2 whole, which is shorter than its diff:
```python
import functools
import itertools
import math

import jax
import jax.numpy as jnp
from jax import lax
from jax.experimental import pallas as pl
from jax.experimental.pallas import tpu as pltpu
from jax.sharding import PartitionSpec as P

R = 16
STEPS = 4
D = 2 * STEPS
ROWS, COLS = 64, 128
TOP = 16
BOT = TOP + ROWS
FRAME = 96
MESH = pl.DeviceIdType.MESH


def lanes(rows=8):
    return lax.broadcasted_iota(jnp.int32, (rows, COLS), 1)


def roll(x, shift):
    shift = shift % COLS
    return x if shift == 0 else pltpu.roll(x, shift, axis=x.ndim - 1)


def pick(index, parts):
    out = parts[0]
    for r in range(1, len(parts)):
        out = jnp.where(index == r, parts[r], out)
    return out


def coefficients(ea, no, di):
    e = di + jnp.maximum(-ea, 0.0)
    w = di + jnp.maximum(ea, 0.0)
    n = di + jnp.maximum(-no, 0.0)
    s = di + jnp.maximum(no, 0.0)
    return 1.0 - e - w - n - s, e, w, n, s


def rollrows(x, shift):
    return x if shift % 8 == 0 else pltpu.roll(x, shift % 8, axis=0)


def fold(x, s, t):
    sub, eighth = lax.broadcasted_iota(jnp.int32, (8, COLS), 0), lanes() % 8
    out = x
    for a in (1, 2, 3):
        row = a - 1 if t == 0 else 8 - a
        free = eighth >= 8 - a if s == 0 else eighth < a
        moved = roll(rollrows(x, 2 * a if t == 0 else -2 * a), 8 - a if s == 0 else a - 8)
        out = jnp.where((sub == row) & free, moved, out)
    return out


def unfold(x, s, t):
    sub = lax.broadcasted_iota(jnp.int32, (8, COLS), 0)
    out = x
    for a in (1, 2, 3):
        row = 7 - a if t == 0 else a
        moved = roll(rollrows(x, -2 * a if t == 0 else 2 * a), a - 8 if s == 0 else 8 - a)
        out = jnp.where(sub == row, moved, out)
    return out


class Later:
    def __init__(self, ref):
        self.ref, self.held = ref, []

    def put(self, values):
        self.flush()
        self.held = values

    def flush(self):
        for where, x in self.held:
            self.ref[where] = x
        self.held = []


def gather(sub, now):
    for width in (4, 2, 1):
        low = sub % (2 * width) < width
        now = [jnp.where(low, now[i], now[i + width])
               + jnp.where(low, rollrows(now[i], 8 - width), rollrows(now[i + width], width)) for i in range(width)]
    return now[0]


def stencil(k, v, co, prec, src, items):
    at = v * 8
    mid, up, down = pl.ds(at, 8), pl.ds(at - 1, 8), pl.ds(at + 1, 8)
    c, n, s = co(0, mid), co(3, mid), co(4, mid)
    if k <= STEPS:
        e, w = co(1, mid), co(2, mid)
    else:
        e, w = co(1, up), co(2, down)
    p = prec(mid) if k == STEPS else None
    outs = []
    for d in items:
        f = src(d, mid)
        if k <= STEPS:
            out = c * f + e * src(d, down) + w * src(d, up) + n * roll(f, -1) + s * roll(f, 1)
            if k == STEPS:
                out = p * out
        else:
            out = c * f + e * src(d, up) + w * src(d, down) + roll(n * f, 1) + roll(s * f, -1)
        outs.append((d, mid, out))
    return outs


def sketch_kernel(dims, d_hbm, ea_hbm, no_hbm, di_hbm, pr_hbm, sketch, gram, fd, prm, co, hx, hp, st, sp, sc, ws, wr, ds_, dr, acc,
                  gs, g1, g2, gm, in_sem, xs, xr, ps, pr, ys, yr, ycs, ycr, dgs, dgr, gsend, grecv, osem):
    nx, nzl, nc, ny, nzh = dims
    ngx, ngy = nx * nzl * nc, ny * nzh
    gx, gy = lax.axis_index("gx"), lax.axis_index("gy")
    ix, izl, ic = gx // (nzl * nc), (gx // nc) % nzl, gx % nc
    iy, izh = gy // nzh, gy % nzh
    has = (gy > 0, gy < ngy - 1)
    xm, xp = (gx + ngx - 1) % ngx, (gx + 1) % ngx
    xdev = (xm, xp)
    ydev = (jnp.maximum(gy - 1, 0), jnp.minimum(gy + 1, ngy - 1))

    i1, n1 = (ic * nx + ix) * ny + iy, nc * nx * ny
    i2, n2 = izh * nzl + izl, nzh * nzl

    def member1(j):
        c, x, y = (ic + j[0]) % nc, (ix + j[1]) % nx, (iy + j[2]) % ny
        return {"gx": (x * nzl + izl) * nc + c, "gy": y * nzh + izh}

    def member2(j):
        v = (i2 + j[0]) % n2
        return {"gx": (ix * nzl + v % nzl) * nc + ic, "gy": iy * nzh + v // nzl}

    def far_first(*sizes):
        every = [j for j in itertools.product(*map(range, sizes)) if any(j)]
        return sorted(every, key=lambda j: -sum(min(i, n - i) for i, n in zip(j, sizes)))

    plane, ring = far_first(nc, nx, ny), far_first(n2)

    block = pl.when(gx >= 0)
    barrier = pltpu.get_barrier_semaphore()

    def hello(dev):
        pl.semaphore_signal(barrier, inc=1, device_id=dev, device_id_type=MESH)

    for s in range(2):
        @pl.when(has[s])
        def _():
            hello({"gx": gx, "gy": ydev[s]})
            for t in range(2):
                hello({"gx": xdev[t], "gy": ydev[s]})
    for t in range(2):
        hello({"gx": xdev[t], "gy": gy})

    loads = [pltpu.make_async_copy(d_hbm, fd.at[0, :, pl.ds(TOP, ROWS), :], in_sem.at[0])]
    for a, ref in enumerate((ea_hbm, no_hbm, di_hbm, pr_hbm)):
        loads.append(pltpu.make_async_copy(ref, prm.at[a, pl.ds(TOP, ROWS), :], in_sem.at[a + 1]))
    for c in loads:
        c.start()
    for j in ring:
        hello(member2(j))
    for j in plane:
        hello(member1(j))
    for s in range(2):
        @pl.when(jnp.logical_not(has[s]))
        def _():
            wr[s] = jnp.zeros((80, COLS), jnp.float32)
            for t in range(2):
                dr[s, t] = jnp.zeros((8, COLS), jnp.float32)
    for c in loads:
        c.wait()

    lane = lanes()
    blk = (lane // 32, ((lane + 16) % COLS) // 32)
    halo = (lane % 32 < 8, (lane % 32 >= 8) & (lane % 32 < 16))

    def tile(v):
        return pl.ds(pl.multiple_of(v * 8, 8), 8) if not isinstance(v, int) else pl.ds(v * 8, 8)

    def pack_fields(v, later):
        for q in range(4):
            rolled = [roll(fd[0, q + 4 * r, tile(v), :], 8 + 32 * r) for r in range(4)]
            later.put([((0, 4 * s + q, tile(v), slice(None)), pick(blk[s], rolled)) for s in range(2)])

    def pack_params(v, later):
        for a in range(4):
            rolled = [roll(prm[a, tile(v), :], 8 + 32 * r) for r in range(4)]
            later.put([((s, a, tile(v), slice(None)), pick(blk[s], rolled)) for s in range(2)])

    def main_coefs(v):
        for a, x in enumerate(coefficients(*(prm[b, tile(v), :] for b in range(3)))):
            co[a, tile(v), :] = x

    eighth = (lane % 32) // 8
    later, later_w = Later(st), Later(ws)
    for v in range(TOP // 8, BOT // 8):
        w = pl.ds(v * 8 - TOP, 8)
        packed, out = [[], []], []
        for q in range(4):
            rolled = [roll(fd[0, q + 4 * r, tile(v), :], 8 + 32 * r) for r in range(4)]
            for s in range(2):
                packed[s].append(pick(blk[s], rolled))
        for s in range(2):
            out.append(((s, w, slice(None)), pick(eighth, [roll(packed[s][q], 8 * q - 8 + 8 * s) for q in range(4)])))
        later.put([((0, 4 * s + q, tile(v), slice(None)), packed[s][q]) for s in range(2) for q in range(4)])
        later_w.put(out)
    later.flush()
    later_w.flush()
    wide = [[], []]
    for v in range(TOP // 8, BOT // 8):
        for s in range(2):
            wide[s].append(pick(lane // 8, [roll(prm[a, tile(v), :], 8 * a + 8 * s) for a in range(4)]))
    for s in range(2):
        for h in range(2):
            ws[s, pl.ds(ROWS + 8 * h, 8), :] = pick(lane // 32, [roll(wide[s][2 * g + h], 32 * g) for g in range(4)])
        for t in range(2):
            out = fold(ws[s, pl.ds(56 * t, 8), :], s, t)
            par = fold(wide[s][7 * t], s, t)
            sub = lax.broadcasted_iota(jnp.int32, (8, COLS), 0)
            for i in range(4):
                row, at = (4, i) if t == 0 else (3, 4 + i)
                out = jnp.where((sub == row) & (lane // 32 == i), roll(rollrows(par, row - at), 32 * i), out)
            ds_[s, t] = rollrows(out, 0 if t == 0 else -3)

    partners = 2 + 3 * (has[0].astype(jnp.int32) + has[1].astype(jnp.int32)) + (n1 - 1) + (n2 - 1)
    pl.semaphore_wait(barrier, partners)

    def remote(src, dst, s_sem, r_sem, dev):
        return pltpu.make_async_remote_copy(src_ref=src, dst_ref=dst, send_sem=s_sem, recv_sem=r_sem, device_id=dev,
                                            device_id_type=MESH)

    def ycopies(s):
        dev = {"gx": gx, "gy": ydev[s]}
        few, rows, rest = pl.ds(0, 5), pl.ds(0, ROWS), pl.ds(ROWS, 16)
        return [remote(ws.at[s, rest], wr.at[1 - s, rest], ycs.at[s], ycr.at[1 - s], dev)] + [
            remote(ds_.at[s, t, few], dr.at[1 - s, 1 - t, few], dgs.at[s, t], dgr.at[1 - s, 1 - t],
                   {"gx": xdev[t], "gy": ydev[s]})
            for t in range(2)
        ] + [remote(ws.at[s, rows], wr.at[1 - s, rows], ys.at[s], yr.at[1 - s], dev)]

    def xcopies(t):
        dev = {"gx": xdev[t], "gy": gy}
        rows = pl.ds(TOP + 56 * t, 8)
        return [remote(fd.at[0, :, rows, :], hx.at[1 - t], xs.at[t], xr.at[1 - t], dev),
                remote(prm.at[:, rows, :], hp.at[1 - t], ps.at[t], pr.at[1 - t], dev)]

    for s in range(2):
        @pl.when(has[s])
        def _():
            for c in ycopies(s):
                c.start()
    for t in range(2):
        for c in xcopies(t):
            c.start()

    later = Later(sp)
    for v in range(TOP // 8, BOT // 8):
        main_coefs(v)
        pack_params(v, later)
    later.flush()

    def main_step(k, v, items):
        got = stencil(k, v, lambda a, rows: co[a, rows, :], lambda rows: prm[3, rows, :],
                      lambda d, rows: fd[k - 1, d, rows, :], items)
        return [((k, d, rows, slice(None)), x) for d, rows, x in got]

    for k in range(1, D + 1):
        def some(g, _):
            later = Later(fd)
            for v in range(TOP // 8, BOT // 8):
                later.put(main_step(k, v, [8 * g + i for i in range(8)]))
            later.flush()
            return 0
        lax.fori_loop(0, R // 8, some, 0)

    for t in range(2):
        for c in xcopies(t):
            c.wait_recv()
    edge = (TOP // 8 - 1, BOT // 8)
    for t in range(2):
        rows = tile(edge[t])
        for d in range(R):
            fd[0, d, rows, :] = hx[t, d]
        for a in range(4):
            prm[a, rows, :] = hp[t, a]
    laters = [Later(sp), Later(st)]
    for t in range(2):
        main_coefs(edge[t])
        pack_params(edge[t], laters[0])
        pack_fields(edge[t], laters[1])
    for later in laters:
        later.flush()
    for k in range(1, D + 1):
        @block
        def _():
            later = Later(fd)
            for v in (1, 2, 9, 10) if k < D else (2, 9):
                for g in range(2):
                    later.put(main_step(k, v, range(8 * g, 8 * g + 8)))
            later.flush()

    rim = (lane < 8) | (lane >= COLS - 8)
    for bi in range(4):
        for bj in range(bi + 1):
            @block
            def _():
                sums = {}
                for v in range(TOP // 8, BOT // 8):
                    left = [jnp.where(rim, 0.0, fd[D, 4 * bi + i, tile(v), :]) for i in range(4)]
                    right = left if bi == bj else [fd[D, 4 * bj + j, tile(v), :] for j in range(4)]
                    for i in range(4):
                        for j in range(4):
                            if bi > bj or i >= j:
                                x = left[i] * right[j]
                                sums[i, j] = sums[i, j] + x if (i, j) in sums else x
                for (i, j), x in sums.items():
                    i, j = 4 * bi + i, 4 * bj + j
                    acc[16 * i + j] = x
                    if i != j:
                        acc[16 * j + i] = x

    sub = lax.broadcasted_iota(jnp.int32, (8, COLS), 0)
    rows = [gather(sub, [acc[8 * g + i] for i in range(8)]) for g in range(32)]
    stacked = jnp.concatenate(rows, axis=0)
    total = lax.dot_general(jnp.ones((8, COLS), jnp.float32), stacked, (((1,), (1,)), ((), ())),
                            precision=lax.Precision.HIGHEST, preferred_element_type=jnp.float32)

    def spread(value, n, index, member, others, slots, which, meanwhile):
        for i in range(2):
            gs[which, pl.ds(i, 1), :] = value[i]
        slots[index] = gs[which]
        copies = [remote(gs.at[which], slots.at[index], gsend.at[which], grecv.at[which], member(j)) for j in others]
        for c in copies:
            c.start()
        meanwhile()
        some = slots.at[pl.ds(0, n - 1)]
        pltpu.make_async_copy(some, some, grecv.at[which]).wait()
        parts = [slots[j] for j in range(n)]
        while len(parts) > 1:
            parts = [parts[j] + parts[j + 1] if j + 1 < len(parts) else parts[j] for j in range(0, len(parts), 2)]
        return parts[0]

    for h in range(2):
        gm[pl.ds(h, 1), :] = total[0:1, COLS * h:COLS * (h + 1)]

    def arrived(which):
        for s in range(2):
            @pl.when(has[s])
            def _():
                for c in ycopies(1 - s)[which]:
                    c.wait_recv()

    arrived(slice(0, 3))
    for s in range(2):
        @block
        def _():
            later = Later(sc)
            for v in range(1, 11):
                if v in edge:
                    t = edge.index(v)
                    x = rollrows(dr[s, t], 0 if t == 1 else 3)
                    y = jnp.zeros((8, COLS), jnp.float32)
                    for i in range(4):
                        row, at = (4, i) if t == 1 else (3, 4 + i)
                        y = jnp.where(sub == at, roll(rollrows(x, at - row), -32 * i), y)
                    y = unfold(y, 1 - s, 1 - t)
                else:
                    g, h = divmod(v - 2, 2)
                    y = roll(wr[s, pl.ds(ROWS + 8 * h, 8), :], -32 * g)
                y = jnp.where(lane < 32, y, 0.0)
                y = y + roll(y, 32)
                y = y + roll(y, 64)
                par = [jnp.where(halo[s], roll(y, 8 * s - 8 * a), sp[s, a, tile(v), :]) for a in range(4)]
                outside = halo[s] & jnp.logical_not(has[s])
                values = [jnp.where(outside, 0.0, x) for x in coefficients(*par[:3])] + [par[3]]
                later.put([((s, a, tile(v), slice(None)), x) for a, x in enumerate(values)])
            later.flush()
    arrived(slice(3, 4))

    @block
    def _():
        later = Later(st)
        for s in range(2):
            for v in range(1, 11):
                if v in edge:
                    t = edge.index(v)
                    x = unfold(rollrows(dr[s, t], 0 if t == 1 else 3), 1 - s, 1 - t)
                else:
                    x = wr[s, pl.ds(v * 8 - TOP, 8), :]
                later.put([((0, 4 * s + q, tile(v), slice(None)),
                            jnp.where(halo[s], roll(x, 8 * s - 8 * q), st[0, 4 * s + q, tile(v), :])) for q in range(4)])
        later.flush()

    for k in range(1, D + 1):
        @block
        def _():
            later = Later(st)
            for v in range(1, 11) if k < D else range(2, 10):
                both = []
                for s in range(2):
                    got = stencil(k, v, lambda a, rows: sc[s, a, rows, :], lambda rows: sc[s, 5, rows, :],
                                  lambda d, rows: st[(k - 1) % 2, d, rows, :], range(4 * s, 4 * s + 4))
                    both += [((k % 2, d, rows, slice(None)), x) for d, rows, x in got]
                later.put(both)
            later.flush()

    def sides(v):
        return [jnp.where(lane % 32 >= 8, st[0, q, tile(v), :], st[0, 4 + q, tile(v), :]) for q in range(4)]

    sums = {}
    for v in range(TOP // 8, BOT // 8):
        here = [jnp.where(lane % 32 < 16, x, 0.0) for x in sides(v)]
        for delta in range(3):
            there = [roll(x, -32 * delta) for x in here]
            for q, q2 in itertools.product(range(4), range(4)):
                if delta == 1 or q <= q2:
                    x, at = here[q] * there[q2], 16 * delta + 4 * q + q2
                    sums[at] = sums[at] + x if at in sums else x
    none = jnp.zeros((8, COLS), jnp.float32)
    products = jnp.concatenate([gather(sub, [sums.get(8 * g + i, none) for i in range(8)]) for g in range(6)], axis=0)
    mine = []
    for h in range(2):
        i, j = (lane + COLS * h) // R, lane % R
        qi, ri, qj, rj = i % 4, i // 4, j % 4, j // 4
        delta = (rj - ri + 4) % 4
        swap = (delta == 3) | ((delta != 1) & (qi > qj))
        index = 16 * jnp.where(delta == 3, 1, delta) + jnp.where(swap, 4 * qj + qi, 4 * qi + qj)
        first = jnp.where(swap, rj, ri)
        pickers = jnp.concatenate([jnp.where(first == g // 4, 1.0, 0.0) for g in range(R)], axis=0)
        each = jnp.dot(products, pickers, precision=lax.Precision.HIGHEST, preferred_element_type=jnp.float32)
        x = none
        for g in range(6):
            x = x + jnp.where(index == sub + 8 * g, each[8 * g:8 * g + 8], 0.0)
        for width in (4, 2, 1):
            x = x + rollrows(x, width)
        mine.append(x[0:1] + gm[pl.ds(h, 1), :])

    def finish():
        @block
        def _():
            later = Later(fd)
            for v in range(TOP // 8, BOT // 8):
                for q, both in enumerate(sides(v)):
                    later.put([((D, q + 4 * r, tile(v), slice(None)),
                                jnp.where(rim, roll(both, -32 * r - 8), fd[D, q + 4 * r, tile(v), :])) for r in range(4)])
            later.flush()
        whole.start()

    whole = pltpu.make_async_copy(fd.at[D, :, pl.ds(TOP, ROWS), :], sketch, osem.at[0])

    one = spread(mine, n1, i1, member1, plane, g1, 0, finish)
    two = spread([one[0:1], one[1:2]], n2, i2, member2, ring, g2, 1, lambda: None)
    gs[2] = two
    given = pltpu.make_async_copy(gs.at[2], gram, osem.at[1])
    given.start()

    for s in range(2):
        @pl.when(has[s])
        def _():
            for c in ycopies(s):
                c.wait_send()
    for t in range(2):
        for c in xcopies(t):
            c.wait_send()
    for which, n, slots in ((0, n1, g1), (1, n2, g2)):
        some = slots.at[pl.ds(0, n - 1)]
        pltpu.make_async_copy(some, some, gsend.at[which]).wait()
    whole.wait()
    given.wait()


def basis_kernel(scale, sketch, gram, basis, factor, two, fac, own, cb, ob, in_sem, out_sem):
    first = pltpu.make_async_copy(gram, two, in_sem.at[0])
    first.start()
    load = pltpu.make_async_copy(sketch, own, in_sem.at[1])
    load.start()
    first.wait()
    sub = lax.broadcasted_iota(jnp.int32, (8, COLS), 0)
    halves = []
    for h in range(2):
        wide_row = jnp.broadcast_to(two[pl.ds(h, 1), :], (8, COLS))
        halves.append(pick(sub, [roll(wide_row, -16 * i) for i in range(8)]))
    m = jnp.concatenate(halves, axis=0)
    lane16, row16 = lanes(R), lax.broadcasted_iota(jnp.int32, (R, COLS), 0)
    m = jnp.where(lane16 < R, m, jnp.where(lane16 - R == row16, 1.0, 0.0))
    columns = [jnp.broadcast_to(m[:, j:j + 1], (R, COLS)) for j in range(R)]
    pivots = jnp.ones((R, COLS), jnp.float32)
    for k in range(R):
        pivot = columns[k][k:k + 1, :]
        pivots = jnp.where(row16 == k, pivot, pivots)
        if k < R - 1:
            times = jnp.where(row16 > k, columns[k] * (1.0 / pivot), 0.0)
            for j in range(k + 1, R):
                columns[j] = columns[j] - times * columns[j][k:k + 1, :]
            m = m - times * m[k:k + 1, :]
    m = m / jnp.sqrt(pivots)
    fac[...] = (jnp.where(lane16 >= row16, m, 0.0) * (1.0 / scale))[:, :R]
    outs = [pltpu.make_async_copy(fac, factor, out_sem.at[4])]
    outs[0].start()
    m = m * scale
    for j in range(R):
        cb[j] = jnp.broadcast_to(m[:, R + j:R + j + 1], (R, COLS))
    load.wait()
    for b in range(4):
        sums = {}
        for j in range(4 * b + 4):
            src = [own[j, pl.ds(8 * v, 8), :] for v in range(8)]
            for i in range(max(j, 4 * b), 4 * b + 4):
                weight = jnp.broadcast_to(cb[j, i:i + 1, :], (8, COLS))
                for v in range(8):
                    x = weight * src[v]
                    sums[i, v] = sums[i, v] + x if (i, v) in sums else x
        for (i, v), x in sums.items():
            ob[i, pl.ds(8 * v, 8), :] = x
        outs.append(pltpu.make_async_copy(ob.at[pl.ds(4 * b, 4)], basis.at[pl.ds(4 * b, 4)], out_sem.at[b]))
        outs[-1].start()
    for c in outs:
        c.wait()


def build(mesh, dims):
    nx, nzl, nc, ny, nzh = dims
    f32 = jnp.float32
    vmem = lambda *shape: pltpu.VMEM(shape, f32)
    dma = lambda *shape: pltpu.SemaphoreType.DMA(shape)
    grid = jax.ShapeDtypeStruct((R, ROWS, COLS), f32)
    hbm = pl.BlockSpec(memory_space=pl.ANY)
    first = pl.pallas_call(
        functools.partial(sketch_kernel, dims),
        name="sketch",
        out_shape=(grid, jax.ShapeDtypeStruct((2, COLS), f32)),
        in_specs=[hbm] * 5,
        out_specs=(hbm, hbm),
        scratch_shapes=[
            vmem(D + 1, R, FRAME, COLS), vmem(4, FRAME, COLS), vmem(5, FRAME, COLS),
            vmem(2, R, 8, COLS), vmem(2, 4, 8, COLS),
            vmem(2, 8, FRAME, COLS), vmem(2, 4, FRAME, COLS), vmem(2, 6, FRAME, COLS),
            vmem(2, 80, COLS), vmem(2, 80, COLS), vmem(2, 2, 8, COLS), vmem(2, 2, 8, COLS),
            vmem(R * R, 8, COLS), vmem(3, 2, COLS), vmem(nc * nx * ny, 2, COLS), vmem(nzh * nzl, 2, COLS), vmem(2, COLS),
            dma(5), dma(2), dma(2), dma(2), dma(2), dma(2), dma(2), dma(2), dma(2), dma(2, 2), dma(2, 2), dma(2), dma(2), dma(2),
        ],
        compiler_params=pltpu.CompilerParams(collective_id=0, has_side_effects=True, vmem_limit_bytes=60 * 2**20),
    )

    def per_device(*args):
        sketch, gram = first(*args)
        scale = math.sqrt(float(ROWS * COLS * nx * nzl * nc * ny * nzh))
        return pl.pallas_call(
            functools.partial(basis_kernel, scale),
            name="basis",
            out_shape=(grid, jax.ShapeDtypeStruct((R, R), f32)),
            in_specs=[hbm, hbm],
            out_specs=(hbm, hbm),
            scratch_shapes=[vmem(2, COLS), vmem(R, R), vmem(R, ROWS, COLS), vmem(R, R, COLS), vmem(R, ROWS, COLS), dma(2), dma(5)],
            compiler_params=pltpu.CompilerParams(vmem_limit_bytes=60 * 2**20),
        )(sketch, gram)

    return jax.shard_map(
        per_device,
        mesh=mesh,
        in_specs=(P(None, "gx", "gy"),) + (P("gx", "gy"),) * 4,
        out_specs=(P(None, "gx", "gy"), P()),
        check_vma=False,
    )


def solution(mesh):
    return build(mesh, (mesh.shape["gx"] // 16, 8, 2, mesh.shape["gy"] // 2, 2))
```

time: 59 us -> 51.5 us (0.87)
  local copies, waits for them, and re-layouts: 5.46 us -> 0 us
  Pallas kernels: 52.4 us -> 50.7 us
    unnamed x12 -> x0, local copies, waits for them, and re-layouts: 5.46 us -> none
    pallas_call x1 -> x2, Pallas kernels: 52.4 us -> 50.7 us  [the longest x1 48.6 us: per_device(): sketch, gram = first(*args)]
where the time goes in v2:
time: 51.5 us; the launch traced here: 51.3 us
  Pallas kernels  50.7 us (98%)
  between operations  0.64 us (1%)
    pallas_call x1, Pallas kernels, per_device(): sketch, gram = first(*args)  48.6 us
    pallas_call x1, Pallas kernels, per_device(): pl.pallas_call(functools.partial(basis_kernel, scale), name='basis', out_...  2.11 us

profile of v2, /device:TPU:1, one launch (start us, length us, event | category | flops | bytes accessed | tf_op | source)
XLA Modules:
  0.0 51.3 jit_solution(4337510689290048307)
XLA Ops:
  0.6 48.6 %sketch.1 = (f32[16,64,128]{2,1,0:T(8,128)}, f32[2,128]{1,0:T(2,128)}) custom-call(f32[16,64,128]{2,1,0:T(8,128)} %d_hbm.1, f32[64,128]{1,0:T(8,128)} %ea_hbm.1, f32[64,128]{1,0:T(8,128)} %no_hbm.1, f32[64,128]{1,0:T(8,128)} %di_hbm.1, f32[64,128]{1,0:T(8,128)} %pr_hbm.1), custom_call_target="tpu_custom_call" | custom-call | tf_op jit(solution)/shard_map/sketch/pallas_call | solution.py:550
  49.2 2.1 %basis.1 = (f32[16,64,128]{2,1,0:T(8,128)}, f32[16,16]{1,0:T(8,128)}) custom-call(f32[16,64,128]{2,1,0:T(8,128)} %get-tuple-element.4.sketch, f32[2,128]{1,0:T(2,128)} %get-tuple-element.5.gram), custom_call_target="tpu_custom_call" | custom-call | tf_op jit(solution)/shard_map/basis/pallas_call | solution.py:552

commit v3 on v2

--- a/solution.py
+++ b/solution.py
@@ -248,14 +248,22 @@
         return [remote(fd.at[0, :, rows, :], hx.at[1 - t], xs.at[t], xr.at[1 - t], dev),
                 remote(prm.at[:, rows, :], hp.at[1 - t], ps.at[t], pr.at[1 - t], dev)]
 
+    wraps = ((izl == 0) & (ic == 0), (izl == nzl - 1) & (ic == nc - 1))
+
+    def send_x(far):
+        for t in range(2):
+            @pl.when(wraps[t] if far else jnp.logical_not(wraps[t]))
+            def _():
+                for c in xcopies(t):
+                    c.start()
+
+    send_x(True)
     for s in range(2):
         @pl.when(has[s])
         def _():
             for c in ycopies(s):
                 c.start()
-    for t in range(2):
-        for c in xcopies(t):
-            c.start()
+    send_x(False)
 
     later = Later(sp)
     for v in range(TOP // 8, BOT // 8):

time: 51.5 us -> 49.7 us (0.965)
  Pallas kernels: 50.7 us -> 48.9 us
    pallas_call x1, Pallas kernels: 48.6 us -> 46.8 us  [per_device(): sketch, gram = first(*args)]
where the time goes in v3:
time: 49.7 us; the launch traced here: 49.6 us
  Pallas kernels  48.9 us (98%)
  between operations  0.64 us (1%)
    pallas_call x1, Pallas kernels, per_device(): sketch, gram = first(*args)  46.8 us
    pallas_call x1, Pallas kernels, per_device(): pl.pallas_call(functools.partial(basis_kernel, scale), name='basis', out_...  2.11 us

profile of v3, /device:TPU:1, one launch (start us, length us, event | category | flops | bytes accessed | tf_op | source)
XLA Modules:
  0.0 49.6 jit_solution(3216428594524007669)
XLA Ops:
  0.6 46.8 %sketch.1 = (f32[16,64,128]{2,1,0:T(8,128)}, f32[2,128]{1,0:T(2,128)}) custom-call(f32[16,64,128]{2,1,0:T(8,128)} %d_hbm.1, f32[64,128]{1,0:T(8,128)} %ea_hbm.1, f32[64,128]{1,0:T(8,128)} %no_hbm.1, f32[64,128]{1,0:T(8,128)} %di_hbm.1, f32[64,128]{1,0:T(8,128)} %pr_hbm.1), custom_call_target="tpu_custom_call" | custom-call | tf_op jit(solution)/shard_map/sketch/pallas_call | solution.py:558
  47.5 2.1 %basis.1 = (f32[16,64,128]{2,1,0:T(8,128)}, f32[16,16]{1,0:T(8,128)}) custom-call(f32[16,64,128]{2,1,0:T(8,128)} %get-tuple-element.4.sketch, f32[2,128]{1,0:T(2,128)} %get-tuple-element.5.gram), custom_call_target="tpu_custom_call" | custom-call | tf_op jit(solution)/shard_map/basis/pallas_call | solution.py:560

commit v4 on v3

--- a/solution.py
+++ b/solution.py
@@ -113,7 +113,7 @@
 
 
 def sketch_kernel(dims, d_hbm, ea_hbm, no_hbm, di_hbm, pr_hbm, sketch, gram, fd, prm, co, hx, hp, st, sp, sc, ws, wr, ds_, dr, acc,
-                  gs, g1, g2, gm, in_sem, xs, xr, ps, pr, ys, yr, ycs, ycr, dgs, dgr, gsend, grecv, osem):
+                  gs, g1, g2, gm, chosen, pickers, in_sem, xs, xr, ps, pr, ys, yr, ycs, ycr, dgs, dgr, gsend, grecv, osem):
     nx, nzl, nc, ny, nzh = dims
     ngx, ngy = nx * nzl * nc, ny * nzh
     gx, gy = lax.axis_index("gx"), lax.axis_index("gy")
@@ -355,6 +355,18 @@
     for h in range(2):
         gm[pl.ds(h, 1), :] = total[0:1, COLS * h:COLS * (h + 1)]
 
+    for h in range(2):
+        i, j = (lane + COLS * h) // R, lane % R
+        qi, ri, qj, rj = i % 4, i // 4, j % 4, j // 4
+        delta = (rj - ri + 4) % 4
+        swap = (delta == 3) | ((delta != 1) & (qi > qj))
+        index = 16 * jnp.where(delta == 3, 1, delta) + jnp.where(swap, 4 * qj + qi, 4 * qi + qj)
+        block_of = jnp.where(swap, rj, ri)
+        for g in range(6):
+            chosen[pl.ds(8 * g, 8), pl.ds(COLS * h, COLS)] = jnp.where(index == sub + 8 * g, 1.0, 0.0)
+        pickers[:, pl.ds(COLS * h, COLS)] = jnp.concatenate(
+            [jnp.where(block_of == g // 4, 1.0, 0.0) for g in range(R)], axis=0).astype(jnp.bfloat16)
+
     def arrived(which):
         for s in range(2):
             @pl.when(has[s])
@@ -430,22 +442,18 @@
                     sums[at] = sums[at] + x if at in sums else x
     none = jnp.zeros((8, COLS), jnp.float32)
     products = jnp.concatenate([gather(sub, [sums.get(8 * g + i, none) for i in range(8)]) for g in range(6)], axis=0)
-    mine = []
-    for h in range(2):
-        i, j = (lane + COLS * h) // R, lane % R
-        qi, ri, qj, rj = i % 4, i // 4, j % 4, j // 4
-        delta = (rj - ri + 4) % 4
-        swap = (delta == 3) | ((delta != 1) & (qi > qj))
-        index = 16 * jnp.where(delta == 3, 1, delta) + jnp.where(swap, 4 * qj + qi, 4 * qi + qj)
-        first = jnp.where(swap, rj, ri)
-        pickers = jnp.concatenate([jnp.where(first == g // 4, 1.0, 0.0) for g in range(R)], axis=0)
-        each = jnp.dot(products, pickers, precision=lax.Precision.HIGHEST, preferred_element_type=jnp.float32)
-        x = none
-        for g in range(6):
-            x = x + jnp.where(index == sub + 8 * g, each[8 * g:8 * g + 8], 0.0)
-        for width in (4, 2, 1):
-            x = x + rollrows(x, width)
-        mine.append(x[0:1] + gm[pl.ds(h, 1), :])
+    high = products.astype(jnp.bfloat16)
+    rest = products - high.astype(jnp.float32)
+    mid = rest.astype(jnp.bfloat16)
+    low = (rest - mid.astype(jnp.float32)).astype(jnp.bfloat16)
+    each = jnp.dot(jnp.concatenate([high, mid, low], axis=0), pickers[...], preferred_element_type=jnp.float32)
+    each = (each[0:48] + each[48:96] + each[96:144]) * chosen[...]
+    x = each[0:8]
+    for g in range(1, 6):
+        x = x + each[8 * g:8 * g + 8]
+    for width in (4, 2, 1):
+        x = x + rollrows(x, width)
+    mine = [x[0:1, COLS * h:COLS * (h + 1)] + gm[pl.ds(h, 1), :] for h in range(2)]
 
     def finish():
         @block
@@ -549,6 +557,7 @@
             vmem(2, 8, FRAME, COLS), vmem(2, 4, FRAME, COLS), vmem(2, 6, FRAME, COLS),
             vmem(2, 80, COLS), vmem(2, 80, COLS), vmem(2, 2, 8, COLS), vmem(2, 2, 8, COLS),
             vmem(R * R, 8, COLS), vmem(3, 2, COLS), vmem(nc * nx * ny, 2, COLS), vmem(nzh * nzl, 2, COLS), vmem(2, COLS),
+            vmem(48, 2 * COLS), pltpu.VMEM((COLS, 2 * COLS), jnp.bfloat16),
             dma(5), dma(2), dma(2), dma(2), dma(2), dma(2), dma(2), dma(2), dma(2), dma(2, 2), dma(2, 2), dma(2), dma(2), dma(2),
         ],
         compiler_params=pltpu.CompilerParams(collective_id=0, has_side_effects=True, vmem_limit_bytes=60 * 2**20),

time: 49.7 us -> 49.6 us (level)
  no operation moved by 1% of the time
where the time goes in v4:
time: 49.6 us; the launch traced here: 49.4 us
  Pallas kernels  48.8 us (98%)
  between operations  0.64 us (1%)
    pallas_call x1, Pallas kernels, per_device(): sketch, gram = first(*args)  46.7 us
    pallas_call x1, Pallas kernels, per_device(): pl.pallas_call(functools.partial(basis_kernel, scale), name='basis', out_...  2.11 us

profile of v4, /device:TPU:1, one launch (start us, length us, event | category | flops | bytes accessed | tf_op | source)
XLA Modules:
  0.0 49.4 jit_solution(9662213926501115433)
XLA Ops:
  0.6 46.7 %sketch.1 = (f32[16,64,128]{2,1,0:T(8,128)}, f32[2,128]{1,0:T(2,128)}) custom-call(f32[16,64,128]{2,1,0:T(8,128)} %d_hbm.1, f32[64,128]{1,0:T(8,128)} %ea_hbm.1, f32[64,128]{1,0:T(8,128)} %no_hbm.1, f32[64,128]{1,0:T(8,128)} %di_hbm.1, f32[64,128]{1,0:T(8,128)} %pr_hbm.1), custom_call_target="tpu_custom_call" | custom-call | tf_op jit(solution)/shard_map/sketch/pallas_call | solution.py:567
  47.3 2.1 %basis.1 = (f32[16,64,128]{2,1,0:T(8,128)}, f32[16,16]{1,0:T(8,128)}) custom-call(f32[16,64,128]{2,1,0:T(8,128)} %get-tuple-element.4.sketch, f32[2,128]{1,0:T(2,128)} %get-tuple-element.5.gram), custom_call_target="tpu_custom_call" | custom-call | tf_op jit(solution)/shard_map/basis/pallas_call | solution.py:569
